TPU v7x, 32 devices: a whole 2x2x4 slice. The times are simulated.
32 devices in a mesh: dp: 2 (over x), seq: 8 (over z, y), mp: 2 (over core).
Axes of the slice: x: 2, y: 2, z: 4, core: 2. Of those that a mesh axis runs over, the one named last changes fastest.
Arguments:
- inputs: bfloat16 [6144, 1024], P(('dp', 'seq')), may hold values from -6 to 6
- doc_lengths: int32 [2, 2], P('dp'), may hold values from 1 to 3072, as said below
- slopes: float32 [8], P('mp'), as said below
- norm_gain: float32 [2, 1024], replicated, may hold values from 0.25 to 1.75
- norm_bias: float32 [2, 1024], replicated, may hold values from -4 to 4
- w_qkv: bfloat16 [3, 1024, 1024], P(None, None, 'mp'), may hold values from -0.25 to 0.25
- qv_bias: float32 [2, 1024], P(None, 'mp'), may hold values from -4 to 4
- w_out: bfloat16 [1024, 1024], P('mp'), may hold values from -0.75 to 0.75
- w_up: bfloat16 [1024, 4096], P(None, 'mp'), may hold values from -0.1875 to 0.1875
- up_bias: float32 [4096], P('mp'), may hold values from -4 to 4
- w_down: bfloat16 [4096, 1024], P('mp'), may hold values from -0.09375 to 0.09375
- out_bias: float32 [2, 1024], replicated, may hold values from -4 to 4
- cotangent: bfloat16 [6144, 1024], P(('dp', 'seq')), may hold values from -6 to 6
Outputs:
- outputs: bfloat16 [6144, 1024], P(('dp', 'seq'))
- grad_inputs: float32 [6144, 1024], P(('dp', 'seq'))
- grad_norm_gain: float32 [2, 1024], replicated
- grad_norm_bias: float32 [2, 1024], replicated
- grad_qkv: float32 [3, 1024, 1024], P(None, ('dp', 'seq'), 'mp')
- grad_qv_bias: float32 [2, 1024], P(None, 'mp')
- grad_out: float32 [1024, 1024], P('mp', ('dp', 'seq'))
- grad_up: float32 [1024, 4096], P(('dp', 'seq'), 'mp')
- grad_up_bias: float32 [4096], P('mp')
- grad_down: float32 [4096, 1024], P('mp', ('dp', 'seq'))
- grad_out_bias: float32 [2, 1024], replicated
Inputs may be any that keep to these rules, and one draw needn't show every extreme that they name: `doc_lengths`: each row holds the lengths of the 2 documents of one block, in order; they sum to 3072, and none is longer than min(4096, 3072). `slopes`: every slope is positive.
All inputs are finite; a program needn't handle non-finite values.
Results may differ from a plain program's by a relative error of at most 0.02.
Values may be sent and summed in bfloat16 or wider, within the bound.
No kernel may reach another device: no remote copies, remote signals or barrier semaphores. Data moves between devices by JAX's collectives and lax.ppermute only.
A program may use at most 256 MiB of HBM per device.

v0:
```python
import jax
import jax.numpy as jnp
from jax import lax
from jax.sharding import PartitionSpec as P

D = 1024
HD = 128


norm_eps = 1e-05
masked_fill = -1e30


def layer_norm(values, scale_row, shift_row):
    centered = values - jnp.mean(values, axis=-1, keepdims=True)
    spread = jnp.mean(centered * centered, axis=-1, keepdims=True)
    return centered * lax.rsqrt(spread + norm_eps) * scale_row + shift_row


def doc_index(positions, bounds):
    return jnp.sum((positions[:, None] >= bounds[None, :]).astype(jnp.int32), axis=1)


def tile_scores(query_part, query_pos, query_doc, key_part, key_pos, key_doc, slopes):
    scores = jnp.einsum("hqd,hkd->hqk", query_part, key_part, preferred_element_type=jnp.float32)
    distance = (query_pos[:, None] - key_pos[None, :]).astype(jnp.float32)
    scores = scores - slopes[:, None, None] * distance[None, :, :]
    allowed = (key_pos[None, :] <= query_pos[:, None]) & (key_doc[None, :] == query_doc[:, None])
    return (scores, allowed[None, :, :])


def over_blocks(folder, current, pieces, tok_rows):
    row_count = pieces[0].shape[1]
    factor = 1
    while factor * 2 * tok_rows <= 2048 and row_count % (factor * 2 * tok_rows) == 0:
        factor = factor * 2
    block_rows = factor * tok_rows

    def step_block(number, inner_state):
        offset = number * block_rows
        sliced = tuple(
            (lax.dynamic_slice_in_dim(member, offset, block_rows, 1) for member in pieces)
        )
        return folder(inner_state, sliced, offset)

    return lax.fori_loop(0, row_count // block_rows, step_block, current)


def body(
    inputs,
    doc_lengths,
    slopes,
    norm_gain,
    norm_bias,
    w_qkv,
    qv_bias,
    w_out,
    w_up,
    up_bias,
    w_down,
    out_bias,
    cotangent,
):
    tok_rows = inputs.shape[0]
    heads_here = slopes.shape[0]
    width_here = heads_here * HD
    score_scale = HD ** (-0.5)
    bounds = jnp.cumsum(doc_lengths[0])
    own_pos = lax.axis_index("seq") * tok_rows + jnp.arange(tok_rows, dtype=jnp.int32)
    own_doc = doc_index(own_pos, bounds)
    input_float = inputs.astype(jnp.float32)
    normed_one_f, norm_one_back = jax.vjp(layer_norm, input_float, norm_gain[0], norm_bias[0])
    normed_one = normed_one_f.astype(jnp.bfloat16)
    weight_heads = w_qkv.reshape(3, D, heads_here, HD)
    projected = jnp.einsum(
        "td,jdhe->jhte", normed_one, weight_heads, preferred_element_type=jnp.float32
    )
    bias_heads = qv_bias.reshape(2, heads_here, 1, HD)
    queries = ((projected[0] + bias_heads[0]) * score_scale).astype(jnp.bfloat16)
    key_rows = projected[1].astype(jnp.bfloat16)
    value_rows = (projected[2] + bias_heads[1]).astype(jnp.bfloat16)

    def attend(current, pieces, row_start):
        key_part, value_part = pieces
        key_pos = row_start + jnp.arange(key_part.shape[1], dtype=jnp.int32)
        key_doc = doc_index(key_pos, bounds)
        touches = (key_pos[0] <= own_pos[-1]) & (key_doc[-1] >= own_doc[0])

        def attend_compute(previous):
            running, row_total, summed = previous
            scores, allowed = tile_scores(
                queries, own_pos, own_doc, key_part, key_pos, key_doc, slopes
            )
            row_top = jnp.maximum(running, jnp.max(jnp.where(allowed, scores, masked_fill), axis=2))
            weights = jnp.where(allowed, jnp.exp(scores - row_top[:, :, None]), 0.0)
            rescale = jnp.exp(running - row_top)
            row_total = row_total * rescale + jnp.sum(weights, axis=2)
            summed = summed * rescale[:, :, None] + jnp.einsum(
                "hqk,hkd->hqd",
                weights.astype(jnp.bfloat16),
                value_part,
                preferred_element_type=jnp.float32,
            )
            return (row_top, row_total, summed)

        return lax.cond(touches, attend_compute, lambda previous: previous, current)

    start_state = (
        jnp.full((heads_here, tok_rows), masked_fill, jnp.float32),
        jnp.zeros((heads_here, tok_rows), jnp.float32),
        jnp.zeros((heads_here, tok_rows, HD), jnp.float32),
    )
    running, row_total, summed = over_blocks(
        attend,
        start_state,
        (
            lax.all_gather(key_rows, "seq", axis=1, tiled=True),
            lax.all_gather(value_rows, "seq", axis=1, tiled=True),
        ),
        tok_rows,
    )
    attended_f = summed / row_total[:, :, None]
    log_total = running + jnp.log(row_total)
    attended = attended_f.astype(jnp.bfloat16)
    w_out_heads = w_out.reshape(heads_here, HD, D)
    attn_part = jnp.einsum("hte,hed->td", attended, w_out_heads, preferred_element_type=jnp.float32)
    mixed = (
        input_float
        + lax.psum(attn_part.astype(jnp.bfloat16), "mp").astype(jnp.float32)
        + out_bias[0]
    )
    normed_two_f, norm_two_back = jax.vjp(layer_norm, mixed, norm_gain[1], norm_bias[1])
    normed_two = normed_two_f.astype(jnp.bfloat16)
    hidden = jnp.dot(normed_two, w_up, preferred_element_type=jnp.float32) + up_bias
    active_f, gelu_back = jax.vjp(jax.nn.gelu, hidden)
    active = active_f.astype(jnp.bfloat16)
    ffn_part = jnp.dot(active, w_down, preferred_element_type=jnp.float32)
    outputs = (
        mixed + lax.psum(ffn_part.astype(jnp.bfloat16), "mp").astype(jnp.float32) + out_bias[1]
    ).astype(jnp.bfloat16)
    contract_rows = (((0,), (0,)), ((), ()))
    contract_cols = (((1,), (1,)), ((), ()))
    grad_float = cotangent.astype(jnp.float32)
    grad_low = grad_float.astype(jnp.bfloat16)
    grad_down = lax.dot_general(active, grad_low, contract_rows, preferred_element_type=jnp.float32)
    grad_active = lax.dot_general(
        grad_low, w_down, contract_cols, preferred_element_type=jnp.float32
    )
    grad_hidden = gelu_back(grad_active)[0].astype(jnp.bfloat16)
    grad_up = lax.dot_general(
        normed_two, grad_hidden, contract_rows, preferred_element_type=jnp.float32
    )
    back_two = lax.dot_general(grad_hidden, w_up, contract_cols, preferred_element_type=jnp.float32)
    grad_normed_two = lax.psum(back_two.astype(jnp.bfloat16), "mp").astype(jnp.float32)
    grad_mixed, gain_two, shift_two = norm_two_back(grad_normed_two)
    grad_mid = grad_float + grad_mixed
    grad_mid_low = grad_mid.astype(jnp.bfloat16)
    grad_out = jnp.einsum(
        "hte,td->hed", attended, grad_mid_low, preferred_element_type=jnp.float32
    ).reshape(width_here, D)
    grad_attended = jnp.einsum(
        "td,hed->hte", grad_mid_low, w_out_heads, preferred_element_type=jnp.float32
    ).astype(jnp.bfloat16)
    row_delta = jnp.sum(grad_attended.astype(jnp.float32) * attended_f, axis=2)

    def query_grad(current, pieces, row_start):
        key_part, value_part = pieces
        key_pos = row_start + jnp.arange(key_part.shape[1], dtype=jnp.int32)
        key_doc = doc_index(key_pos, bounds)
        touches = (key_pos[0] <= own_pos[-1]) & (key_doc[-1] >= own_doc[0])

        def query_compute(grad_sum):
            scores, allowed = tile_scores(
                queries, own_pos, own_doc, key_part, key_pos, key_doc, slopes
            )
            probabilities = jnp.where(allowed, jnp.exp(scores - log_total[:, :, None]), 0.0)
            grad_probs = jnp.einsum(
                "hqd,hkd->hqk", grad_attended, value_part, preferred_element_type=jnp.float32
            )
            grad_scores = (probabilities * (grad_probs - row_delta[:, :, None])).astype(
                jnp.bfloat16
            )
            return grad_sum + jnp.einsum(
                "hqk,hkd->hqd", grad_scores, key_part, preferred_element_type=jnp.float32
            )

        return lax.cond(touches, query_compute, lambda grad_sum: grad_sum, current)

    zero_heads = jnp.zeros((heads_here, tok_rows, HD), jnp.float32)
    grad_queries = over_blocks(
        query_grad,
        zero_heads,
        (
            lax.all_gather(key_rows, "seq", axis=1, tiled=True),
            lax.all_gather(value_rows, "seq", axis=1, tiled=True),
        ),
        tok_rows,
    )
    all_log_total, all_delta = (
        lax.all_gather(log_total, "seq", axis=1, tiled=True),
        lax.all_gather(row_delta, "seq", axis=1, tiled=True),
    )

    def key_grad(current, pieces, row_start):
        query_part, grad_part = pieces
        row_count = query_part.shape[1]
        query_pos = row_start + jnp.arange(row_count, dtype=jnp.int32)
        query_doc = doc_index(query_pos, bounds)
        touches = (own_pos[0] <= query_pos[-1]) & (own_doc[-1] >= query_doc[0])

        def key_compute(grad_pair):
            key_sum, value_sum = grad_pair
            scores, allowed = tile_scores(
                query_part, query_pos, query_doc, key_rows, own_pos, own_doc, slopes
            )
            part_total = lax.dynamic_slice_in_dim(all_log_total, row_start, row_count, 1)
            part_delta = lax.dynamic_slice_in_dim(all_delta, row_start, row_count, 1)
            probabilities = jnp.where(allowed, jnp.exp(scores - part_total[:, :, None]), 0.0)
            value_sum = value_sum + jnp.einsum(
                "hqk,hqd->hkd",
                probabilities.astype(jnp.bfloat16),
                grad_part,
                preferred_element_type=jnp.float32,
            )
            grad_probs = jnp.einsum(
                "hqd,hkd->hqk", grad_part, value_rows, preferred_element_type=jnp.float32
            )
            grad_scores = (probabilities * (grad_probs - part_delta[:, :, None])).astype(
                jnp.bfloat16
            )
            key_sum = key_sum + jnp.einsum(
                "hqk,hqd->hkd", grad_scores, query_part, preferred_element_type=jnp.float32
            )
            return (key_sum, value_sum)

        return lax.cond(touches, key_compute, lambda grad_pair: grad_pair, current)

    grad_keys, grad_values = over_blocks(
        key_grad,
        (zero_heads, zero_heads),
        (
            lax.all_gather(queries, "seq", axis=1, tiled=True),
            lax.all_gather(grad_attended, "seq", axis=1, tiled=True),
        ),
        tok_rows,
    )
    grad_three = jnp.stack(
        [
            grad_queries.astype(jnp.bfloat16),
            grad_keys.astype(jnp.bfloat16),
            grad_values.astype(jnp.bfloat16),
        ]
    )
    back_three = jnp.einsum(
        "jhte,jdhe->jtd", grad_three, weight_heads, preferred_element_type=jnp.float32
    )
    back_one = back_three[0] * score_scale + back_three[1] + back_three[2]
    grad_normed_one = lax.psum(back_one.astype(jnp.bfloat16), "mp").astype(jnp.float32)
    grad_input_norm, gain_one, shift_one = norm_one_back(grad_normed_one)
    grad_inputs = grad_mid + grad_input_norm
    scale_three = jnp.array([score_scale, 1.0, 1.0], jnp.float32)[:, None, None, None]
    grad_heads = jnp.einsum(
        "td,jhte->jdhe", normed_one, grad_three, preferred_element_type=jnp.float32
    )
    grad_qkv = (grad_heads * scale_three).reshape(3, D, width_here)
    grad_qv_bias = jnp.stack(
        [
            jnp.sum(grad_three[0].astype(jnp.float32), axis=1) * score_scale,
            jnp.sum(grad_three[2].astype(jnp.float32), axis=1),
        ]
    ).reshape(2, width_here)
    grad_gain = jnp.stack([gain_one, gain_two])
    grad_shift = jnp.stack([shift_one, shift_two])
    grad_out_bias = jnp.stack(
        [
            jnp.sum(grad_mid_low.astype(jnp.float32), axis=0),
            jnp.sum(grad_low.astype(jnp.float32), axis=0),
        ]
    )
    grad_up_bias = jnp.sum(grad_hidden.astype(jnp.float32), axis=0)
    small_sums = lax.psum(
        (grad_gain, grad_shift, grad_qv_bias, grad_up_bias, grad_out_bias), ("dp", "seq")
    )
    weight_sums = (
        lax.psum_scatter(grad_qkv, ("dp", "seq"), scatter_dimension=1, tiled=True),
        lax.psum_scatter(grad_out, ("dp", "seq"), scatter_dimension=1, tiled=True),
        lax.psum_scatter(grad_up, ("dp", "seq"), scatter_dimension=0, tiled=True),
        lax.psum_scatter(grad_down, ("dp", "seq"), scatter_dimension=1, tiled=True),
    )
    return (
        outputs,
        grad_inputs,
        small_sums[0],
        small_sums[1],
        weight_sums[0],
        small_sums[2],
        weight_sums[1],
        weight_sums[2],
        small_sums[3],
        weight_sums[3],
        small_sums[4],
    )


def solution(mesh):
    return jax.shard_map(
        body,
        mesh=mesh,
        in_specs=(
            P(("dp", "seq"), None),
            P("dp", None),
            P("mp"),
            P(),
            P(),
            P(None, None, "mp"),
            P(None, "mp"),
            P("mp", None),
            P(None, "mp"),
            P("mp"),
            P("mp", None),
            P(),
            P(("dp", "seq"), None),
        ),
        out_specs=(
            P(("dp", "seq"), None),
            P(("dp", "seq"), None),
            P(),
            P(),
            P(None, ("dp", "seq"), "mp"),
            P(None, "mp"),
            P("mp", ("dp", "seq")),
            P(("dp", "seq"), "mp"),
            P("mp"),
            P("mp", ("dp", "seq")),
            P(),
        ),
        check_vma=False,
    )
```

profile of v0, /device:TPU:0, one launch (start us, length us, event | category | flops | bytes accessed | tf_op | source)
XLA Modules:
  0.0 1064.4 jit_solution(10984702625545935948)
XLA Ops:
  7.2 1.5 convert_reduce_fusion.3
  8.7 1.5 fusion.96
  13.7 2.6 fusion.90
  18.8 1.9 slice.183
  22.3 59.8 %all-gather.6.cloned.1.call-done = bf16[4,3072,128]{2,1,0:T(8,128)(2,1)} async-done(((bf16[4,384,128]{2,1,0:T(8,128)(2,1)}), bf16[4,3072,128]{2,1,0:T(8,128)(2,1)}) %all-gather.6.cloned.1.call-update) | async-done | bytes 3145744 | tf_op jit(solution)/shard_map/all_gather | solution.py:118
  82.2 61.9 %all-gather.12.cloned.1.call-done = bf16[1,4,3072,128]{3,2,1,0:T(8,128)(2,1)} async-done(((bf16[1,4,384,128]{3,2,1,0:T(8,128)(2,1)}), bf16[1,4,3072,128]{3,2,1,0:T(8,128)(2,1)}) %all-gather.12.cloned.1.call-update) | async-done | bytes 3145744 | tf_op jit(solution)/shard_map/all_gather | solution.py:117
  146.2 31.8 %while.48 = (s32[]{:T(128)}, f32[4,384]{1,0:T(4,128)}, f32[4,384]{1,0:T(4,128)}, f32[4,384,128]{2,1,0:T(8,128)}, s32[384]{0:T(512)S(1)}, /*index=5*/s32[2]{0:T(1...) while((s32[]{:T(128)}, f32[4,384]{1,0:T(4,128)}, ...), condition=%wide.region_10.11_spmd, body=%wide.region_4.10_spmd.sunk | while | flops 1244344320 | bytes 89474240 | solution.py:46
  153.0 18.1 %conditional.6 = ((f32[4,384]{1,0:T(4,128)}, f32[4,384]{1,0:T(4,128)}, f32[4,384,128]{2,1,0:T(8,128)})) conditional(s32[]{:T(128)} %bitcast.142, (f32[4,384]{1,0:T(4,128)}, f32[4,384]{1,0:T(4,128)}, f32[4,384,128]{2,1,0:T(8,128)}) %tuple.152, (s32[1536]{0:T(1024)S(1)}, s32[384]{0:T(512)S(1)}, s32[1536]{0:T(1024)}, s32[384]{0:T(512)S(1)}, s32[]{:T(128)}, ...), branch_computations={%region_6.6_spmd, %region_7.9_spmd} | conditional | flops 1244335104 | bytes 89455480 | solution.py:106
  153.4 2.0 compare_and_fusion
  155.4 3.6 select_reduce_fusion
  159.0 2.5 fusion.1
  162.6 7.0 fusion.8
  178.1 2.4 copy.41
  180.5 3.0 bitcast_convert_fusion
  184.6 6.0 fusion.138
  190.6 29.0 %all-reduce.6.cloned.1.call-done = bf16[384,1024]{1,0:T(8,128)(2,1)} async-done(((bf16[384,1024]{1,0:T(8,128)(2,1)}), bf16[384,1024]{1,0:T(8,128)(2,1)}) %all-reduce.6.cloned.1.call-update) | async-done | bytes 786448 | tf_op jit(solution)/shard_map/psum | solution.py:129
  219.6 1.8 fusion.104
  221.4 1.8 multiply_reduce_fusion
  223.3 9.2 convert_reduce_fusion
  233.6 2.7 convolution_convert_fusion
  236.4 20.5 %all-reduce.8.cloned.1.call-done = bf16[384,1024]{1,0:T(8,128)(2,1)} async-done(((bf16[384,1024]{1,0:T(8,128)(2,1)}), bf16[384,1024]{1,0:T(8,128)(2,1)}) %all-reduce.8.cloned.1.call-update) | async-done | bytes 786448 | tf_op jit(solution)/shard_map/psum | solution.py:154
  256.9 3.0 convert_reduce_fusion.2
  260.0 1.6 fusion.99
  261.6 1.4 convert_reduce_fusion.5
  263.0 2.1 multiply_reduce_fusion.1
  265.8 1.9 slice_bitcast_fusion.2
  267.7 32.2 %all_gather.23 = f32[4,3072]{1,0:T(4,128)} all-gather(f32[4,384]{1,0:T(4,128)S(1)} %log_add_fusion), channel_id=1, replica_groups=mesh['dp'=2,'seq'=8,'mp'=2] {'seq'}, dimensions={1}, use_global_device_ids=true | all-gather | bytes 55296 | tf_op jit(solution)/shard_map/all_gather | solution.py:200
  300.0 6.3 convolution_convert_fusion.1
  306.2 2.0 copy.43
  308.2 32.4 %all_gather.25 = f32[4,3072]{1,0:T(4,128)} all-gather(f32[4,384]{1,0:T(4,128)} %get-tuple-element.1576), channel_id=1, replica_groups=mesh['dp'=2,'seq'=8,'mp'=2] {'seq'}, dimensions={1}, use_global_device_ids=true | all-gather | bytes 55296 | tf_op jit(solution)/shard_map/all_gather | solution.py:201
  341.7 35.7 %while.49 = (s32[]{:T(128)}, f32[4,384,128]{2,1,0:T(8,128)}, s32[384]{0:T(512)S(1)}, s32[2]{0:T(128)}, s32[384]{0:T(512)S(1)}, /*index=5*/bf16[4,3072,128]{2,1,0...) while((s32[]{:T(128)}, f32[4,384,128]{2,1,0:T(8,128)}, ...), condition=%wide.region_23.24_spmd, body=%wide.region_19.0_spmd.sunk | while | flops 1831609344 | bytes 31906156 | solution.py:46
  348.6 21.7 %conditional.7 = (f32[4,384,128]{2,1,0:T(8,128)}) conditional(s32[]{:T(128)} %bitcast.143, f32[4,384,128]{2,1,0:T(8,128)} %get-tuple-element.1580, (s32[1536]{0:T(1024)S(1)}, s32[384]{0:T(512)S(1)}, s32[1536]{0:T(1024)}, s32[384]{0:T(512)S(1)}, s32[]{:T(128)}, /*index=5*/bf16[4,3072,128]{2,1,0:T(8,128)(2,1)}, bf16[4,384,128]{2,1,0:T(8,128)(2,1)S(1)}, ...), branch_computations={%region_21.21_spmd, %region_22.22_spmd} | conditional | flops 1831600128 | bytes 31887406 | solution.py:187
  348.7 6.4 fusion.26
  355.1 1.7 subtract_convert_fusion.1
  356.8 2.1 compare_and_fusion.1
  358.9 11.5 %fusion.28 = f32[4,384,128]{2,1,0:T(8,128)} fusion(f32[4,384,128]{2,1,0:T(8,128)} %get-tuple-element.994, bf16[4,3072,128]{2,1,0:T(8,128)(2,1)} %get-tuple-element.999, s32[]{:T(128)S(6)} %select_n.58, f32[4,1536,384]{1,2,0:T(8,128)} %fusion.26, bf16[4,384,128]{2,1,0:T(8,128)(2,1)} %get-tuple-element.1005, f32[4,384]{1,0:T(4,128)} %get-tuple-element.1006, ...), kind=kOutput, calls=%fused_computation.34 | convolution fusion | flops 1224671232 | bytes 17511936 | tf_op jit(solution)/shard_map/while/body/eval_jaxpr/cond/branch_1_fun/hqk,hkd->hqd/dot_general | solution.py:183
  377.4 4.7 copy.44
  382.1 9.6 all-gather.8.cloned.1.call-done
  393.7 55.7 %while.50 = (s32[]{:T(128)}, f32[4,384,128]{2,1,0:T(8,128)}, f32[4,384,128]{2,1,0:T(8,128)}, s32[384]{0:T(512)S(1)}, s32[384]{0:T(512)S(1)}, /*index=5*/s32[2]{0...) while((s32[]{:T(128)}, f32[4,384,128]{2,1,0:T(8,128)}, ...), condition=%wide.region_28.29_spmd, body=%wide.region_24.0_spmd.sunk | while | flops 2447582208 | bytes 116509552 | solution.py:46
  400.7 20.9 %conditional.8 = ((f32[4,384,128]{2,1,0:T(8,128)}, f32[4,384,128]{2,1,0:T(8,128)})) conditional(s32[]{:T(128)} %bitcast.144, (f32[4,384,128]{2,1,0:T(8,128)}, f32[4,384,128]{2,1,0:T(8,128)}) %tuple.157, (s32[384]{0:T(512)S(1)}, s32[1536]{0:T(1024)S(1)}, s32[384]{0:T(512)S(1)}, s32[1536]{0:T(1024)}, s32[]{:T(128)}, ...), branch_computations={%region_26.26_spmd, %region_27.27_spmd} | conditional | flops 2447572992 | bytes 116490768 | solution.py:236
  400.8 3.0 fusion.47
  404.7 2.0 compare_and_fusion.2
  406.8 4.3 fusion.49
  412.0 9.7 fusion.54
  428.5 20.9 %conditional.8 = ((f32[4,384,128]{2,1,0:T(8,128)}, f32[4,384,128]{2,1,0:T(8,128)})) conditional(s32[]{:T(128)} %bitcast.144, (f32[4,384,128]{2,1,0:T(8,128)}, f32[4,384,128]{2,1,0:T(8,128)}) %tuple.157, (s32[384]{0:T(512)S(1)}, s32[1536]{0:T(1024)S(1)}, s32[384]{0:T(512)S(1)}, s32[1536]{0:T(1024)}, s32[]{:T(128)}, ...), branch_computations={%region_26.26_spmd, %region_27.27_spmd} | conditional | flops 2447572992 | bytes 116490768 | solution.py:236
  428.5 2.9 fusion.47
  432.4 2.0 compare_and_fusion.2
  434.5 4.3 fusion.49
  439.8 9.7 fusion.54
  450.6 2.2 convert_reduce_fusion.6
  454.3 1.4 fusion.107
  455.9 3.4 fusion.114
  459.3 3.2 copy.48
  462.9 7.7 fusion.125
  470.6 8.1 fusion.128
  479.4 6.1 broadcast_multiply_fusion
  485.5 6.6 copy.47
  492.8 2.0 convert_reduce_fusion.1
  494.9 2.3 fusion.100
  497.3 3.9 add_add_fusion.2
  501.3 73.4 %all-reduce = (f32[2,1024]{1,0:T(2,128)}, f32[2,1024]{1,0:T(2,128)}, f32[2,512]{1,0:T(2,128)}, f32[2048]{0:T(1024)}, f32[2,1024]{1,0:T(2,128)}) all-reduce(f32[2,1024]{1,0:T(2,128)S(1)} %pad_maximum_fusion.3, f32[2,1024]{1,0:T(2,128)S(1)} %pad_maximum_fusion.4, ...), channel_id=1, replica_groups=mesh['dp'=2,'seq'=8,'mp'=2] {'dp','seq'}, use_global_device_ids=true, to_apply=%region_34.35 | all-reduce | flops 9216 | bytes 73728 | tf_op jit(solution)/shard_map/psum | solution.py:281
  574.6 162.9 %reduce-scatter.9.cloned.1.call-done = f32[64,2048]{1,0:T(8,128)} async-done(((f32[1024,2048]{1,0:T(8,128)}), f32[64,2048]{1,0:T(8,128)}) %reduce-scatter.9.cloned.1.call-update) | async-done | bytes 524304 | tf_op jit(solution)/shard_map/reduce_scatter | solution.py:287
  737.5 180.4 %reduce-scatter.11.cloned.1.call-done = f32[2048,64]{0,1:T(8,128)} async-done(((f32[2048,1024]{0,1:T(8,128)}), f32[2048,64]{0,1:T(8,128)}) %reduce-scatter.11.cloned.1.call-update) | async-done | bytes 524304 | tf_op jit(solution)/shard_map/reduce_scatter | solution.py:288
  918.0 139.5 %reduce-scatter.5.cloned.1.call-done = f32[3,64,512]{2,1,0:T(8,128)} async-done(((f32[3,1024,512]{2,1,0:T(8,128)}), f32[3,64,512]{2,1,0:T(8,128)}) %reduce-scatter.5.cloned.1.call-update) | async-done | bytes 393232 | tf_op jit(solution)/shard_map/reduce_scatter | solution.py:285
  (277 shorter events, 52.3 us)
Async XLA Ops:
  7.2 6.6 copy-start
  7.2 75.0 %all-gather.6.cloned.1.call-start = ((), (), s32[]{:S(2)}) async-start(), calls=%async_computation.4 | async-start | bytes 3538944 | tf_op jit(solution)/shard_map/all_gather | solution.py:118
  8.7 7.7 copy-start.50
  10.2 3.5 copy-start.62
  10.2 6.2 copy-start.57
  11.6 4.8 copy-start.44
  16.4 4.4 copy-start.76
  18.8 125.3 %all-gather.12.cloned.1.call-start = ((), (), s32[]{:S(2)}) async-start(), calls=%async_computation.13 | async-start | bytes 3538944 | tf_op jit(solution)/shard_map/all_gather | solution.py:117
  20.8 198.8 %all-reduce.6.cloned.1.call-start = ((), (), s32[]{:S(2)}) async-start(), calls=%async_computation.5 | async-start | bytes 1572864 | tf_op jit(solution)/shard_map/psum | solution.py:129
  155.4 3.6 copy-start.27
  159.0 3.6 copy-start.1
  159.0 3.6 copy-start.38
  159.0 3.6 copy-start.19
  162.6 7.1 copy-start.39
  178.0 5.4 copy-start.6
  183.5 73.4 %all-reduce.8.cloned.1.call-start = ((), (), s32[]{:S(2)}) async-start(), calls=%async_computation.6 | async-start | bytes 1572864 | tf_op jit(solution)/shard_map/psum | solution.py:154
  184.6 76.9 %copy-start.34 = (f32[1,1024]{1,0:T(1,128)}, f32[1,1024]{1,0:T(1,128)S(1)}, u32[]{:S(2)}) copy-start(f32[1,1024]{1,0:T(1,128)S(1)} %get-tuple-element.1230) | copy-start | bytes 12292
  190.6 32.7 %copy-start.36 = (f32[1,1024]{1,0:T(1,128)S(1)}, f32[1,1024]{1,0:T(1,128)}, u32[]{:S(2)}) copy-start(f32[1,1024]{1,0:T(1,128)} %get-tuple-element.1232) | copy-start | bytes 12292
  190.6 32.7 %copy-start.46 = (f32[1,1024]{1,0:T(1,128)S(1)}, f32[1,1024]{1,0:T(1,128)}, u32[]{:S(2)}) copy-start(f32[1,1024]{1,0:T(1,128)} %get-tuple-element.1234) | copy-start | bytes 12292
  190.6 32.7 %copy-start.75 = (f32[2048]{0:T(1024)S(1)}, f32[2048]{0:T(1024)}, u32[]{:S(2)}) copy-start(f32[2048]{0:T(1024)} %param.35) | copy-start | bytes 24580
  219.6 3.7 copy-start.3
  219.6 3.7 copy-start.9
  221.4 40.1 %copy-start.42 = (f32[384]{0:T(512)}, f32[384]{0:T(512)S(1)}, u32[]{:S(2)}) copy-start(f32[384]{0:T(512)S(1)} %broadcast_multiply_fusion.2) | copy-start | bytes 4612
  223.2 38.3 %copy-start.48 = (f32[384]{0:T(512)}, f32[384]{0:T(512)S(1)}, u32[]{:S(2)}) copy-start(f32[384]{0:T(512)S(1)} %fusion.122) | copy-start | bytes 4612
  223.3 10.3 copy-start.73
  236.4 141.0 %all-gather.10.cloned.1.call-start = ((), (), s32[]{:S(2)}) async-start(), calls=%async_computation.8 | async-start | bytes 3538944 | tf_op jit(solution)/shard_map/all_gather | solution.py:243
  256.9 4.6 copy-start.17
  261.6 3.6 copy-start.60
  263.0 4.7 copy-start.28
  265.2 126.6 %all-gather.8.cloned.1.call-start = ((), (), s32[]{:S(2)}) async-start(), calls=%async_computation.7 | async-start | bytes 3538944 | tf_op jit(solution)/shard_map/all_gather | solution.py:242
  265.7 227.0 %all-reduce.10.cloned.1.call-start = ((), (), s32[]{:S(2)}) async-start(), calls=%async_computation.14 | async-start | bytes 3145728 | tf_op jit(solution)/shard_map/psum | solution.py:139
  267.7 32.2 %copy-start.59 = (f32[4,384]{1,0:T(4,128)}, f32[4,384]{1,0:T(4,128)S(1)}, u32[]{:S(2)}) copy-start(f32[4,384]{1,0:T(4,128)S(1)} %log_add_fusion) | copy-start | bytes 18436
  300.0 41.7 %copy-start.7 = (bf16[4,384,128]{2,1,0:T(8,128)(2,1)S(1)}, bf16[4,384,128]{2,1,0:T(8,128)(2,1)}, u32[]{:S(2)}) copy-start(bf16[4,384,128]{2,1,0:T(8,128)(2,1)} %copy-done.6) | copy-start | bytes 1179652
  377.4 16.3 %copy-start.12 = (bf16[4,384,128]{2,1,0:T(8,128)(2,1)S(1)}, bf16[4,384,128]{2,1,0:T(8,128)(2,1)}, u32[]{:S(2)}) copy-start(bf16[4,384,128]{2,1,0:T(8,128)(2,1)} %slice_bitcast_fusion.2) | copy-start | bytes 1179652
  400.8 6.0 copy-start.18
  403.7 7.4 copy-start.2
  404.4 6.7 copy-start.31
  404.7 6.4 copy-start.8
  406.7 4.4 copy-start.13
  406.8 5.2 copy-start.54
  428.5 6.0 copy-start.18
  431.5 7.4 copy-start.2
  432.2 6.7 copy-start.31
  432.4 6.4 copy-start.8
  434.5 4.4 copy-start.13
  434.5 5.2 copy-start.54
  450.6 3.7 copy-start.25
  455.8 118.9 %reduce-scatter.7.cloned.1.call-start = ((), (), s32[]{:S(2)}) async-start(), calls=%async_computation.10 | async-start | bytes 2228224 | tf_op jit(solution)/shard_map/reduce_scatter | solution.py:286
  459.3 3.5 copy-start.47
  462.5 275.0 %reduce-scatter.9.cloned.1.call-start = ((), (), s32[]{:S(2)}) async-start(), calls=%async_computation.11 | async-start | bytes 8912896 | tf_op jit(solution)/shard_map/reduce_scatter | solution.py:287
  470.6 447.4 %reduce-scatter.11.cloned.1.call-start = ((), (), s32[]{:S(2)}) async-start(), calls=%async_computation.12 | async-start | bytes 8912896 | tf_op jit(solution)/shard_map/reduce_scatter | solution.py:288
  478.8 578.7 %reduce-scatter.5.cloned.1.call-start = ((), (), s32[]{:S(2)}) async-start(), calls=%async_computation.9 | async-start | bytes 6684672 | tf_op jit(solution)/shard_map/reduce_scatter | solution.py:285
  492.1 5.1 copy-start.49
  492.1 5.1 copy-start.56
  492.1 5.1 copy-start.61
  492.1 5.1 copy-start.65
  492.8 4.5 copy-start.5
  492.8 4.5 copy-start.11
  492.8 4.5 copy-start.15
  492.8 4.5 copy-start.16
  497.3 3.9 copy-start.68
  497.3 3.9 copy-start.66
  497.3 3.9 copy-start.67
  497.3 4.0 copy-start.72
  (35 other events, 79.5 us)
Sparse Core Ops, SparseCore 0:
  18.9 63.2 all-gather.5
  84.9 59.1 all-gather.11
  183.6 35.9 all-reduce.5
  236.5 20.3 all-reduce.7
  265.3 65.0 all-gather.9
  333.0 58.7 all-gather.7
  455.9 18.5 all-reduce.9
  477.5 82.0 reduce-scatter.6
  562.5 174.9 reduce-scatter.8
  740.4 177.5 reduce-scatter.10
  920.9 136.4 reduce-scatter.4
where the time goes:
time: 1070 us; the launch traced here: 1060 us
  waiting for transfers between devices  664 us (62%)
  blocking collectives  138 us (13%)
  matrix products  121 us (11%)
  local copies, waits for them, and re-layouts  59.1 us (6%)
  other arithmetic  49.3 us (5%)
  loops' own time  16.5 us (2%)
  between operations  15 us (1%)
    reduce_scatter x1, waiting for transfers between devices, body(): lax.psum_scatter(grad_down, ('dp', 'seq'), scatter_dimension=1, tiled=True)  180 us
    reduce_scatter x1, waiting for transfers between devices, body(): lax.psum_scatter(grad_up, ('dp', 'seq'), scatter_dimension=0, tiled=True)  163 us
    reduce_scatter x1, waiting for transfers between devices, body(): lax.psum_scatter(grad_qkv, ('dp', 'seq'), scatter_dimension=1, tiled=True)  139 us
    psum x1, blocking collectives, body(): lax.psum((grad_gain, grad_shift, grad_qv_bias, grad_up_bias, grad_out_bia...  73.4 us
    all_gather x1, waiting for transfers between devices, body(): lax.all_gather(key_rows, 'seq', axis=1, tiled=True)  61.9 us
    all_gather x1, waiting for transfers between devices, body(): lax.all_gather(value_rows, 'seq', axis=1, tiled=True)  59.8 us
    all_gather x1, blocking collectives, body(): lax.all_gather(row_delta, 'seq', axis=1, tiled=True)  32.4 us
    all_gather x1, blocking collectives, body(): lax.all_gather(log_total, 'seq', axis=1, tiled=True)  32.2 us
  transfers between devices with their start and end apart: 11, of which 8 were waited for; matrix products, arithmetic and copies ran while one was open for 9% of the time, Pallas kernels for 0%

commit v1 on v0

v1 whole, which is shorter than its diff:
```python
import functools

import jax
import jax.numpy as jnp
from jax import lax
from jax.experimental import pallas as pl
from jax.experimental.pallas import tpu as pltpu
from jax.sharding import Mesh
from jax.sharding import PartitionSpec as P

D = 1024
HD = 128
BF16 = jnp.bfloat16
F32 = jnp.float32

norm_eps = 1e-05
masked_fill = -1e30

NT = (((1,), (1,)), ((), ()))
NN = (((1,), (0,)), ((), ()))
TN = (((0,), (0,)), ((), ()))


def mm(a, b, dims=NN):
    return lax.dot_general(a, b, dims, preferred_element_type=F32)


def doc_start(docs_ref, position):
    start = jnp.zeros_like(position)
    bound = jnp.int32(0)
    for d in range(docs_ref.shape[1]):
        bound = bound + docs_ref[0, d]
        start = jnp.where(position >= bound, bound, start)
    return start


def natural_order(place_ref, own, others, groups, cols, store):
    me, col = place_ref[0], place_ref[1]
    for k in range(groups):
        z = lax.rem(me + (groups - k), groups)
        store(z, z * cols + col, own[k], True)
        for s in range(1, cols):
            there = lax.rem(col + (cols - s), cols)
            store(z, z * cols + there, others[s - 1][k], False)


def bias_tile(slope, tok):
    rows = lax.broadcasted_iota(jnp.int32, (tok, tok), 0)
    lanes = lax.broadcasted_iota(jnp.int32, (tok, tok), 1)
    return slope * (rows - lanes).astype(F32)


def valid_tile(docs_ref, key_base, query_base, tok):
    keys = key_base + lax.broadcasted_iota(jnp.int32, (tok, tok), 0)
    queries = query_base + lax.broadcasted_iota(jnp.int32, (1, tok), 1)
    return (keys <= queries) & (keys >= doc_start(docs_ref, queries))


def forward_kernel(groups, cols, tok, place_ref, docs_ref, slope_ref, *refs):
    n_other = (cols - 1) * groups
    own = refs[:groups]
    others = [refs[groups + s * groups : groups + (s + 1) * groups] for s in range(cols - 1)]
    refs = refs[groups + n_other :]
    outs, (ot_ref, lse_ref), scratch = refs[:groups], refs[groups : groups + 2], refs[groups + 2 :]
    q_s, k_s, vt_s, bias_s, acc_s = scratch
    me, col = place_ref[0], place_ref[1]
    slope = slope_ref[0]

    def store(z, block, piece, mine):
        if mine:
            q_s[z] = piece[0]
            k_s[block] = piece[1]
            vt_s[block] = piece[2].T
        else:
            k_s[block] = piece[0]
            vt_s[block] = piece[1].T

    natural_order(place_ref, own, others, groups, cols, store)
    bias_s[...] = bias_tile(slope, tok)
    for k in range(groups):
        z = lax.rem(me + k, groups)
        block = z * cols + col
        query = q_s[z]
        first = doc_start(docs_ref, block * tok)
        last = doc_start(docs_ref, block * tok + tok - 1)
        low = first // tok
        mid = jnp.clip((last + tok - 1) // tok, low, block)

        scores = mm(k_s[block], query, NT) + bias_s[...]
        scores = jnp.where(valid_tile(docs_ref, block * tok, block * tok, tok), scores, masked_fill)
        top = jnp.max(scores, axis=0, keepdims=True)
        weights = jnp.exp(scores - top)
        total = jnp.sum(weights, axis=0, keepdims=True)
        acc_s[...] = mm(vt_s[block], weights.astype(BF16))

        def step(kb, state, masked):
            top, total = state
            shift = slope * ((kb - block) * tok).astype(F32)
            scores = mm(k_s[kb], query, NT) + bias_s[...] + shift
            if masked:
                scores = jnp.where(
                    valid_tile(docs_ref, kb * tok, block * tok, tok), scores, masked_fill
                )
            new_top = jnp.maximum(top, jnp.max(scores, axis=0, keepdims=True))
            weights = jnp.exp(scores - new_top)
            rescale = jnp.exp(top - new_top)
            total = total * rescale + jnp.sum(weights, axis=0, keepdims=True)
            acc_s[...] = acc_s[...] * rescale + mm(vt_s[kb], weights.astype(BF16))
            return (new_top, total)

        state = (top, total)
        state = lax.fori_loop(low, mid, functools.partial(step, masked=True), state)
        top, total = lax.fori_loop(mid, block, functools.partial(step, masked=False), state)
        result = acc_s[...] / total
        ot_ref[z] = result
        lse_ref[z] = top + jnp.log(total)
        outs[k][...] = result.T.astype(BF16)


def backward_kernel(groups, cols, tok, place_ref, docs_ref, slope_ref, *refs):
    n_other = (cols - 1) * groups
    own = refs[:groups]
    others = [refs[groups + s * groups : groups + (s + 1) * groups] for s in range(cols - 1)]
    refs = refs[groups + n_other :]
    grads, (ot_ref, lse_ref) = refs[:groups], refs[groups : groups + 2]
    dq_refs = refs[groups + 2 : 2 * groups + 2]
    own_ref = refs[2 * groups + 2]
    refs = refs[2 * groups + 3 :]
    if cols > 1:
        other_ref, refs = refs[0], refs[1:]
    q_s, k_s, v_s, kt_s, do_s, delta_s, bias_s, dk_s, dv_s, dqt_s = refs
    me, col = place_ref[0], place_ref[1]
    slope = slope_ref[0]

    def store(z, block, piece, mine):
        if mine:
            q_s[z] = piece[0]
        key, value = (piece[1], piece[2]) if mine else (piece[0], piece[1])
        k_s[block] = key
        v_s[block] = value
        kt_s[block] = key.T

    natural_order(place_ref, own, others, groups, cols, store)
    for k in range(groups):
        z = lax.rem(me + k, groups)
        grad = grads[k][...]
        do_s[z] = grad
        delta_s[z] = jnp.sum(grad.astype(F32).T * ot_ref[z], axis=0, keepdims=True)
    bias_s[...] = bias_tile(slope, tok)
    dqt_s[...] = jnp.zeros_like(dqt_s)

    def over_keys(kb, carry):
        z_key, col_key = kb // cols, lax.rem(kb, cols)
        first_query = z_key + (col_key > col).astype(jnp.int32)
        dk_s[...] = jnp.zeros_like(dk_s)
        dv_s[...] = jnp.zeros_like(dv_s)

        def tile(z, masked):
            block = z * cols + col
            shift = slope * ((kb - block) * tok).astype(F32)
            query, grad = q_s[z], do_s[z]
            scores = mm(k_s[kb], query, NT) + bias_s[...]
            probs = jnp.exp(scores - (lse_ref[z] - shift))
            if masked:
                probs = jnp.where(valid_tile(docs_ref, kb * tok, block * tok, tok), probs, 0.0)
            dv_s[...] += mm(probs.astype(BF16), grad)
            grad_probs = mm(v_s[kb], grad, NT)
            grad_scores = (probs * (grad_probs - delta_s[z])).astype(BF16)
            dk_s[...] += mm(grad_scores, query)
            dqt_s[z] += mm(kt_s[kb], grad_scores)

        def over_queries(z, carry):
            block = z * cols + col
            first = doc_start(docs_ref, block * tok)
            last = doc_start(docs_ref, block * tok + tok - 1)
            touches = first < (kb + 1) * tok
            masked = (block == kb) | (last > kb * tok)

            @pl.when(touches & masked)
            def _():
                tile(z, True)

            @pl.when(touches & jnp.logical_not(masked))
            def _():
                tile(z, False)

            return carry

        lax.fori_loop(first_query, groups, over_queries, 0)
        k = lax.rem(z_key - me + groups, groups)
        s = lax.rem(col - col_key + cols, cols)

        @pl.when(s == 0)
        def _():
            own_ref[k, 0] = dk_s[...]
            own_ref[k, 1] = dv_s[...]

        if cols > 1:

            @pl.when(s != 0)
            def _():
                other_ref[s - 1, k, 0] = dk_s[...].astype(BF16)
                other_ref[s - 1, k, 1] = dv_s[...].astype(BF16)

        return carry

    lax.fori_loop(0, groups * cols, over_keys, 0)
    for k in range(groups):
        z = lax.rem(me + k, groups)
        dq_refs[k][...] = (dqt_s[z] * (HD**-0.5)).T.astype(BF16)


SMEM = pl.BlockSpec(memory_space=pltpu.SMEM)
VMEM = pl.BlockSpec(memory_space=pltpu.VMEM)
VMEM_BYTES = 60 * 2**20


def attend_forward(place, docs, slope, own, others, groups, cols, tok):
    flat = list(own) + [piece for column in others for piece in column]
    blocks = groups * cols
    out_shape = [jax.ShapeDtypeStruct((tok, HD), BF16)] * groups + [
        jax.ShapeDtypeStruct((groups, HD, tok), F32),
        jax.ShapeDtypeStruct((groups, 1, tok), F32),
    ]
    results = pl.pallas_call(
        functools.partial(forward_kernel, groups, cols, tok),
        out_shape=out_shape,
        in_specs=[SMEM] * 3 + [VMEM] * len(flat),
        out_specs=[VMEM] * len(out_shape),
        scratch_shapes=[
            pltpu.VMEM((groups, tok, HD), BF16),
            pltpu.VMEM((blocks, tok, HD), BF16),
            pltpu.VMEM((blocks, HD, tok), BF16),
            pltpu.VMEM((tok, tok), F32),
            pltpu.VMEM((HD, tok), F32),
        ],
        compiler_params=pltpu.CompilerParams(vmem_limit_bytes=VMEM_BYTES),
        cost_estimate=pl.CostEstimate(
            flops=2 * blocks * groups * tok * tok * HD,
            bytes_accessed=2 * (groups + 2 * blocks) * tok * HD,
            transcendentals=blocks * groups * tok * tok // 2,
        ),
        name="attend_forward",
    )(place, docs, slope, *flat)
    return results[:groups], results[groups], results[groups + 1]


def attend_backward(place, docs, slope, own, others, grads, ot, lse, groups, cols, tok):
    flat = list(own) + [piece for column in others for piece in column]
    blocks = groups * cols
    out_shape = [jax.ShapeDtypeStruct((tok, HD), BF16)] * groups + [
        jax.ShapeDtypeStruct((groups, 2, tok, HD), F32)
    ]
    if cols > 1:
        out_shape.append(jax.ShapeDtypeStruct((cols - 1, groups, 2, tok, HD), BF16))
    results = pl.pallas_call(
        functools.partial(backward_kernel, groups, cols, tok),
        out_shape=out_shape,
        in_specs=[SMEM] * 3 + [VMEM] * (len(flat) + groups + 2),
        out_specs=[VMEM] * len(out_shape),
        scratch_shapes=[
            pltpu.VMEM((groups, tok, HD), BF16),
            pltpu.VMEM((blocks, tok, HD), BF16),
            pltpu.VMEM((blocks, tok, HD), BF16),
            pltpu.VMEM((blocks, HD, tok), BF16),
            pltpu.VMEM((groups, tok, HD), BF16),
            pltpu.VMEM((groups, 1, tok), F32),
            pltpu.VMEM((tok, tok), F32),
            pltpu.VMEM((tok, HD), F32),
            pltpu.VMEM((tok, HD), F32),
            pltpu.VMEM((groups, HD, tok), F32),
        ],
        compiler_params=pltpu.CompilerParams(vmem_limit_bytes=VMEM_BYTES),
        cost_estimate=pl.CostEstimate(
            flops=5 * blocks * groups * tok * tok * HD,
            bytes_accessed=2 * (groups + 4 * blocks) * tok * HD,
            transcendentals=blocks * groups * tok * tok // 2,
        ),
        name="attend_backward",
    )(place, docs, slope, *flat, *grads, ot, lse)
    return results[:groups], results[groups], (results[groups + 1] if cols > 1 else None)


def shift(x, axis, size, k):
    return lax.ppermute(x, axis, [(i, (i + k) % size) for i in range(size)])


def swap_sum(partial):
    low = partial.astype(BF16)
    other = shift(low, "mp", 2, 1)
    return low.astype(F32) + other.astype(F32)


def pair(axis, size, bit):
    return [(i, i ^ bit) for i in range(size)]


def scatter_stages(sizes):
    n_dp, groups, cols = sizes
    stages = []
    for axis, size in (("dp", n_dp), ("sr", cols), ("sg", groups)):
        bit = 1
        while bit < size:
            stages.append((axis, size, bit))
            bit *= 2
    return stages


def scatter_rows(partial_of, sizes):
    n_dp, groups, cols = sizes
    here = {axis: lax.axis_index(axis) for axis in ("dp", "sg", "sr")}
    kept = partial_of(here["dp"])
    if n_dp > 1:
        for k in range(1, n_dp):
            sent = partial_of(lax.rem(here["dp"] + k, n_dp)).astype(BF16)
            kept = kept + shift(sent, "dp", n_dp, k).astype(F32)
    width = kept.shape[1]
    kept = kept.reshape(groups, cols, -1, width)
    dims = {"sg": 0, "sr": 1}
    for axis, size, bit in scatter_stages((1, groups, cols)):
        dim = dims[axis]
        extent = kept.shape
        now = (here[axis] // bit) % 2
        split = extent[:dim] + (extent[dim] // 2, 2) + extent[dim + 1 :]
        view = kept.reshape(split)
        mine = lax.dynamic_index_in_dim(view, now, dim + 1, keepdims=False)
        sent = lax.dynamic_index_in_dim(view, 1 - now, dim + 1, keepdims=False).astype(BF16)
        kept = mine + lax.ppermute(sent, axis, pair(axis, size, bit)).astype(F32)
    return kept.reshape(-1, width)


def sum_all(vector, sizes):
    for axis, size, bit in scatter_stages(sizes):
        vector = vector + lax.ppermute(vector, axis, pair(axis, size, bit))
    return vector


def layer_norm(values, scale_row, shift_row):
    centered = values - jnp.mean(values, axis=-1, keepdims=True)
    spread = jnp.mean(centered * centered, axis=-1, keepdims=True)
    return centered * lax.rsqrt(spread + norm_eps) * scale_row + shift_row


def body(
    sizes,
    inputs,
    doc_lengths,
    slopes,
    norm_gain,
    norm_bias,
    w_qkv,
    qv_bias,
    w_out,
    w_up,
    up_bias,
    w_down,
    out_bias,
    cotangent,
):
    n_dp, groups, cols = sizes
    tok = inputs.shape[0]
    heads = slopes.shape[0]
    width = heads * HD
    me = lax.axis_index("sg")
    col = lax.axis_index("sr")
    place = jnp.stack([me, col]).astype(jnp.int32)
    slope = lax.dynamic_slice_in_dim(slopes, me, 1, 0)
    score_scale = HD ** (-0.5)

    arrive = jnp.remainder(me - jnp.arange(heads), heads)

    input_float = inputs.astype(F32)
    normed_one_f, norm_one_back = jax.vjp(layer_norm, input_float, norm_gain[0], norm_bias[0])
    normed_one = normed_one_f.astype(BF16)
    projected = jnp.einsum(
        "td,jdhe->hjte", normed_one, w_qkv.reshape(3, D, heads, HD), preferred_element_type=F32
    )
    bias_heads = qv_bias.reshape(2, heads, HD).transpose(1, 0, 2)
    bias_three = jnp.stack([bias_heads[:, 0], jnp.zeros_like(bias_heads[:, 0]), bias_heads[:, 1]], 1)
    scale_three = jnp.array([score_scale, 1.0, 1.0], F32)[None, :, None, None]
    three = ((projected + bias_three[:, :, None, :]) * scale_three).astype(BF16)

    own = []
    for k in range(groups):
        piece = lax.dynamic_index_in_dim(three, lax.rem(me + k, groups), 0, keepdims=False)
        own.append(shift(piece, "sg", groups, k) if k else piece)
    others = [[shift(piece[1:], "sr", cols, s) for piece in own] for s in range(1, cols)]
    outs, ot, lse = attend_forward(
        place, doc_lengths, slope, own, others, groups, cols, tok
    )
    back = [shift(outs[k], "sg", groups, k) if k else outs[k] for k in range(groups)]

    def natural(pieces):
        return jnp.take(jnp.stack(pieces), arrive, axis=0).transpose(1, 0, 2).reshape(tok, width)

    attended = natural(back)
    attn_part = mm(attended, w_out)
    mixed = input_float + swap_sum(attn_part) + out_bias[0]
    normed_two_f, norm_two_back = jax.vjp(layer_norm, mixed, norm_gain[1], norm_bias[1])
    normed_two = normed_two_f.astype(BF16)
    hidden = mm(normed_two, w_up) + up_bias
    active_f, gelu_back = jax.vjp(jax.nn.gelu, hidden)
    active = active_f.astype(BF16)
    outputs = (mixed + swap_sum(mm(active, w_down)) + out_bias[1]).astype(BF16)

    grad_low = cotangent
    grad_float = cotangent.astype(F32)
    grad_hidden = gelu_back(mm(grad_low, w_down, NT))[0].astype(BF16)
    grad_mixed, gain_two, shift_two = norm_two_back(swap_sum(mm(grad_hidden, w_up, NT)))
    grad_mid = grad_float + grad_mixed
    grad_mid_low = grad_mid.astype(BF16)
    grad_attended = mm(grad_mid_low, w_out, NT).astype(BF16)
    grads = []
    for k in range(groups):
        head = lax.rem(me - k + heads, heads)
        piece = lax.dynamic_slice_in_dim(grad_attended, head * HD, HD, 1)
        grads.append(shift(piece, "sg", groups, groups - k) if k else piece)

    def rows_of(left, right):
        step = D // n_dp

        def partial_of(index):
            return mm(lax.dynamic_slice_in_dim(left, index * step, step, 1), right, TN)

        return partial_of

    grad_up = scatter_rows(rows_of(normed_two, grad_hidden), sizes)
    grad_down = scatter_rows(rows_of(grad_low, active), sizes).T
    grad_out = scatter_rows(rows_of(grad_mid_low, attended), sizes).T
    small = jnp.concatenate(
        [
            gain_two,
            shift_two,
            jnp.sum(grad_mid_low.astype(F32), axis=0),
            jnp.sum(grad_low.astype(F32), axis=0),
            jnp.sum(grad_hidden.astype(F32), axis=0),
        ]
    )
    small = sum_all(small, sizes)

    dq, dkv, dkv_other = attend_backward(
        place, doc_lengths, slope, own, others, grads, ot, lse, groups, cols, tok
    )
    for s in range(1, cols):
        dkv = dkv + shift(dkv_other[s - 1], "sr", cols, cols - s).astype(F32)
    dkv = dkv.astype(BF16)
    dq_back = [shift(dq[k], "sg", groups, k) if k else dq[k] for k in range(groups)]
    dkv_back = [shift(dkv[k], "sg", groups, k) if k else dkv[k] for k in range(groups)]
    grad_three = jnp.concatenate(
        [natural(dq_back)]
        + [natural([piece[role] for piece in dkv_back]) for role in (0, 1)],
        axis=1,
    )
    w_three = w_qkv.transpose(1, 0, 2).reshape(D, 3 * width)
    grad_input_norm, gain_one, shift_one = norm_one_back(swap_sum(mm(grad_three, w_three, NT)))
    grad_inputs = grad_mid + grad_input_norm
    grad_qkv = scatter_rows(rows_of(normed_one, grad_three), sizes)
    grad_qkv = grad_qkv.reshape(-1, 3, width).transpose(1, 0, 2)
    column_sums = jnp.sum(grad_three.astype(F32), axis=0).reshape(3, width)
    small_two = sum_all(
        jnp.concatenate([gain_one, shift_one, column_sums[0], column_sums[2]]), sizes
    )
    grad_qv_bias = small_two[2 * D :].reshape(2, width)
    return (
        outputs,
        grad_inputs,
        jnp.stack([small_two[:D], small[:D]]),
        jnp.stack([small_two[D : 2 * D], small[D : 2 * D]]),
        grad_qkv,
        grad_qv_bias,
        grad_out,
        grad_up,
        small[4 * D :],
        grad_down,
        jnp.stack([small[2 * D : 3 * D], small[3 * D : 4 * D]]),
    )


def solution(mesh):
    n_dp, n_seq, n_mp = mesh.shape["dp"], mesh.shape["seq"], mesh.shape["mp"]
    groups = 4
    cols = n_seq // groups
    inner = Mesh(mesh.devices.reshape(n_dp, groups, cols, n_mp), ("dp", "sg", "sr", "mp"))
    rows = ("dp", "sg", "sr")
    return jax.shard_map(
        functools.partial(body, (n_dp, groups, cols)),
        mesh=inner,
        in_specs=(
            P(rows, None),
            P("dp", None),
            P("mp"),
            P(),
            P(),
            P(None, None, "mp"),
            P(None, "mp"),
            P("mp", None),
            P(None, "mp"),
            P("mp"),
            P("mp", None),
            P(),
            P(rows, None),
        ),
        out_specs=(
            P(rows, None),
            P(rows, None),
            P(),
            P(),
            P(None, rows, "mp"),
            P(None, "mp"),
            P("mp", rows),
            P(rows, "mp"),
            P("mp"),
            P("mp", rows),
            P(),
        ),
        check_vma=False,
    )
```

time: 1070 us -> 379 us (0.35)
  waiting for transfers between devices: 664 us -> 188 us
  blocking collectives: 138 us -> 0 us
  matrix products: 121 us -> 40.8 us
  starting transfers between devices: 1.17 us -> 51.9 us
  local copies, waits for them, and re-layouts: 59.1 us -> 30.4 us
  Pallas kernels: 0 us -> 28.6 us
  other arithmetic: 49.3 us -> 29.3 us
  loops' own time: 16.5 us -> 0 us
  between operations: 15 us -> 2.1 us
    reduce_scatter x4 -> x0, waiting for transfers between devices: 483 us -> none  [the longest x1 180 us: body(): lax.psum_scatter(grad_down, ('dp', 'seq'), scatter_dimension=1, tiled=True)]
    ppermute x0 -> x48, waiting for transfers between devices: none -> 188 us  [the longest x8 82 us: sum_all(): vector = vector + lax.ppermute(vector, axis, pair(axis, size, bit))]
    all_gather x4 -> x0, waiting for transfers between devices: 131 us -> none  [the longest x1 61.9 us: body(): lax.all_gather(key_rows, 'seq', axis=1, tiled=True)]
    dot_general x22 -> x16, matrix products: 121 us -> 40.8 us  [the longest x15 37.3 us: mm(): return lax.dot_general(a, b, dims, preferred_element_type=F32)]
    psum x1 -> x0, blocking collectives: 73.4 us -> none  [body(): lax.psum((grad_gain, grad_shift, grad_qv_bias, grad_up_bias, grad_out_bia...]
    all_gather x2 -> x0, blocking collectives: 64.7 us -> none  [the longest x1 32.4 us: body(): lax.all_gather(row_delta, 'seq', axis=1, tiled=True)]
    ppermute x0 -> x48, starting transfers between devices: none -> 51.9 us  [the longest x28 41.2 us: shift(): return lax.ppermute(x, axis, [(i, (i + k) % size) for i in range(size)])]
    psum x3 -> x0, waiting for transfers between devices: 49.5 us -> none  [the longest x1 29 us: body(): lax.psum(attn_part.astype(jnp.bfloat16), 'mp').astype(jnp.float32)]
  transfers between devices with their start and end apart: 11 -> 48, of which waited for: 8 -> 27; matrix products, arithmetic and copies ran while one was open for 9% -> 19% of each run, Pallas kernels for 0% -> 4%
where the time goes in v1:
time: 379 us; the launch traced here: 371 us
  waiting for transfers between devices  188 us (50%)
  starting transfers between devices  51.9 us (14%)
  matrix products  40.8 us (11%)
  local copies, waits for them, and re-layouts  30.4 us (8%)
  other arithmetic  29.3 us (8%)
  Pallas kernels  28.6 us (8%)
    ppermute x8, waiting for transfers between devices, sum_all(): vector = vector + lax.ppermute(vector, axis, pair(axis, size, bit))  82 us
    ppermute x12, waiting for transfers between devices, scatter_rows(): kept = mine + lax.ppermute(sent, axis, pair(axis, size, bit)).astype(F32)  59.8 us
    ppermute x28, waiting for transfers between devices, shift(): return lax.ppermute(x, axis, [(i, (i + k) % size) for i in range(size)])  46.3 us
    ppermute x28, starting transfers between devices, shift(): return lax.ppermute(x, axis, [(i, (i + k) % size) for i in range(size)])  41.2 us
    dot_general x15, matrix products, mm(): return lax.dot_general(a, b, dims, preferred_element_type=F32)  37.3 us
    pallas_call x1, Pallas kernels, attend_backward(): pl.pallas_call(functools.partial(backward_kernel, groups, cols, tok), out...  16.4 us
    pallas_call x1, Pallas kernels, attend_forward(): pl.pallas_call(functools.partial(forward_kernel, groups, cols, tok), out_...  12.2 us
    unnamed x102, local copies, waits for them, and re-layouts  9.75 us
  transfers between devices with their start and end apart: 48, of which 27 were waited for; matrix products, arithmetic and copies ran while one was open for 19% of the time, Pallas kernels for 4%

profile of v1, /device:TPU:0, one launch (start us, length us, event | category | flops | bytes accessed | tf_op | source)
XLA Modules:
  0.0 371.2 jit_solution(516235897942722657)
XLA Ops:
  4.3 3.5 fusion.15
  8.7 3.0 collective-permute-start
  11.8 2.6 collective-permute-start.1
  15.7 1.6 collective-permute-start.3
  17.9 4.2 %collective-permute-done.refs_1_ = bf16[3,384,128]{2,1,0:T(8,128)(2,1)} collective-permute-done((bf16[3,384,128]{2,1,0:T(8,128)(2,1)}, bf16[3,384,128]{2,1,0:T(8,128)(2,1)}, u32[]{:S(2)}, u32[]{:S(2)}) %collective-permute-start) | collective-permute-done | bytes 294944 | tf_op jit(solution)/shard_map/ppermute | solution.py:285
  23.0 1.8 collective-permute-start.4
  24.9 9.0 %collective-permute-done.1.refs_2_ = bf16[3,384,128]{2,1,0:T(8,128)(2,1)} collective-permute-done((bf16[3,384,128]{2,1,0:T(8,128)(2,1)}, bf16[3,384,128]{2,1,0:T(8,128)(2,1)}, u32[]{:S(2)}, u32[]{:S(2)}) %collective-permute-start.1) | collective-permute-done | bytes 294944 | tf_op jit(solution)/shard_map/ppermute | solution.py:285
  34.8 1.6 collective-permute-start.5
  38.6 4.1 %collective-permute-done.5.refs_6_ = bf16[2,384,128]{2,1,0:T(8,128)(2,1)S(1)} collective-permute-done((bf16[2,384,128]{2,1,0:T(8,128)(2,1)S(1)}, bf16[2,384,128]{2,1,0:T(8,128)(2,1)S(1)}, u32[]{:S(2)}, u32[]{:S(2)}) %collective-permute-start.5) | collective-permute-done | bytes 196640 | tf_op jit(solution)/shard_map/ppermute | solution.py:285
  42.7 3.2 collective-permute-done.6.refs_7_
  46.5 12.2 %attend_forward.1 = (bf16[384,128]{1,0:T(8,128)(2,1)}, bf16[384,128]{1,0:T(8,128)(2,1)}, bf16[384,128]{1,0:T(8,128)(2,1)}, bf16[384,128]{1,0:T(8,128)(2,1)}, f32...) custom-call(s32[2]{0:T(128)} %pad_add_fusion.place_ref, s32[1,2]{1,0:T(1,128)} %docs_ref.3, f32[1]{0:T(128)} %dynamic_slice.117.slope_ref, ...), custom_call_target="tpu_custom_call" | custom-call | flops 1207959552 | bytes 1966080 | tf_op jit(solution)/shard_map/attend_forward/pallas_call | solution.py:225
  58.7 4.0 %collective-permute-start.7 = (bf16[384,128]{1,0:T(8,128)(2,1)}, bf16[384,128]{1,0:T(8,128)(2,1)S(1)}, u32[]{:S(2)}, u32[]{:S(2)}) collective-permute-start(bf16[384,128]{1,0:T(8,128)(2,1)} %get-tuple-element.25), channel_id=1, source_target_pairs={{0,4},{4,8},{8,12},{12,0},{1,5},{5,9},{9,13},{13,1},{2,6},{6,10},{... | collective-permute-start | bytes 294920 | tf_op jit(solution)/shard_map/ppermute | solution.py:285
  62.8 3.3 collective-permute-start.8
  66.3 2.8 collective-permute-done.7
  69.1 2.8 collective-permute-done.8
  75.6 4.7 %copy.46 = bf16[3,1024,512]{1,2,0:T(8,128)(2,1)} copy(bf16[3,1024,512]{2,1,0:T(8,128)(2,1)} %param.21) | data formatting | bytes 6291456 | tf_op args[5]
  80.3 4.0 %fusion.86 = f32[384,2048]{1,0:T(8,128)S(1)} fusion(bf16[384,1024]{1,0:T(8,128)(2,1)S(1)} %copy-done.10, bf16[2048,1024]{1,0:T(8,128)(2,1)} %param.26), kind=kOutput, calls=%fused_computation.186 | convolution fusion | flops 1610612736 | bytes 8126464 | tf_op jit(solution)/shard_map/dot_general | solution.py:25
  84.4 2.0 fusion.74
  87.4 4.5 %convert_reduce_fusion = (f32[2048]{0:T(1024)}, bf16[384,2048]{1,0:T(8,128)(2,1)S(1)}, f32[384,2048]{1,0:T(8,128)S(1)}) fusion(f32[384,2048]{1,0:T(8,128)S(1)} %fusion.86, f32[2048]{0:T(1024)S(1)} %copy-done.43, bf16[384,1024]{1,0:T(8,128)(2,1)S(1)} %add_convert_fusion.2, bf16[1024,2048]{1,0:T(8,128)(2,1)S(1)} %copy-done.31), kind=kOutput, calls=%fused_computation.19 | convolution fusion | flops 1628698624 | bytes 12861440 | tf_op jit(solution)/shard_map/dot_general | solution.py:25
  91.9 1.8 convolution_convert_fusion.4
  94.3 1.5 copy-done.32
  95.8 2.1 convolution_convert_fusion.5
  98.5 2.9 convolution_convert_fusion
  101.4 2.6 convolution_convert_fusion.1
  104.8 1.8 fusion.73
  108.9 1.5 collective-permute-start.36
  111.7 2.5 collective-permute-start.13
  114.8 2.6 collective-permute-done.13.refs_9_
  117.4 6.2 %collective-permute-done.14.refs_10_ = bf16[384,128]{1,0:T(8,128)(2,1)S(1)} collective-permute-done((bf16[384,128]{1,0:T(8,128)(2,1)S(1)}, bf16[384,128]{1,0:T(8,128)(2,1)S(1)}, u32[]{:S(2)}, u32[]{:S(2)}) %collective-permute-start.14) | collective-permute-done | bytes 98336 | tf_op jit(solution)/shard_map/ppermute | solution.py:285
  124.3 16.4 %attend_backward.1 = (bf16[384,128]{1,0:T(8,128)(2,1)}, bf16[384,128]{1,0:T(8,128)(2,1)}, bf16[384,128]{1,0:T(8,128)(2,1)}, bf16[384,128]{1,0:T(8,128)(2,1)}, f3...) custom-call(s32[2]{0:T(128)} %pad_add_fusion.place_ref, s32[1,2]{1,0:T(1,128)} %docs_ref.3, ...), custom_call_target="tpu_custom_call" | custom-call | flops 3019898880 | bytes 3538944 | tf_op jit(solution)/shard_map/attend_backward/pallas_call | solution.py:256
  140.8 6.9 %collective-permute-start.19 = (bf16[4,2,384,128]{3,2,1,0:T(8,128)(2,1)}, bf16[4,2,384,128]{3,2,1,0:T(8,128)(2,1)}, u32[]{:S(2)}, u32[]{:S(2)}) collective-permute-start(bf16[4,2,384,128]{3,2,1,0:T(8,128)(2,1)} %bitcast.226), channel_id=1, source_target_pairs={{0,2},{2,0},{1,3},{3,1},{4,6},{6,4},{5,7},{7,5},{8,10},{10,8},{9,1... | collective-permute-start | bytes 2359304 | tf_op jit(solution)/shard_map/ppermute | solution.py:285
  147.6 1.6 convert_add_fusion.7
  150.1 1.8 collective-permute-start.17
  151.9 2.5 collective-permute-start.18
  154.4 3.2 collective-permute-done.16
  158.1 2.0 collective-permute-done.17
  161.5 2.3 gather_fusion.1
  163.9 6.9 %collective-permute-done.37 = bf16[4,1,64,512]{3,2,0,1:T(8,128)(2,1)} collective-permute-done((bf16[4,1,64,512]{3,2,0,1:T(8,128)(2,1)}, bf16[4,1,64,512]{3,2,0,1:T(8,128)(2,1)}, u32[]{:S(2)}, u32[]{:S(2)}) %collective-permute-start.37) | collective-permute-done | bytes 262176 | tf_op jit(solution)/shard_map/ppermute | solution.py:328
  173.3 3.6 collective-permute-done.38
  178.0 2.0 collective-permute-start.21
  180.0 9.2 %collective-permute-done.39 = bf16[1,1,64,512]{3,2,0,1:T(8,128)(2,1)S(1)} collective-permute-done((bf16[1,1,64,512]{3,2,0,1:T(8,128)(2,1)S(1)}, bf16[1,1,64,512]{3,2,0,1:T(8,128)(2,1)S(1)}, u32[]{:S(2)}, u32[]{:S(2)}) %collective-permute-start.39) | collective-permute-done | bytes 65568 | tf_op jit(solution)/shard_map/ppermute | solution.py:328
  190.1 4.6 %collective-permute-done.21 = bf16[2,384,128]{2,1,0:T(8,128)(2,1)S(1)} collective-permute-done((bf16[2,384,128]{2,1,0:T(8,128)(2,1)S(1)}, bf16[2,384,128]{2,1,0:T(8,128)(2,1)S(1)}, u32[]{:S(2)}, u32[]{:S(2)}) %collective-permute-start.21) | collective-permute-done | bytes 196640 | tf_op jit(solution)/shard_map/ppermute | solution.py:285
  197.0 1.6 gather_fusion.3
  198.6 2.3 gather_fusion.2
  200.9 2.1 select_bitcast_fusion.2
  205.5 1.9 copy.45
  207.4 3.5 convolution_convert_fusion.3
  211.0 2.2 convolution_convert_fusion.2
  214.4 3.3 convert_add_fusion
  220.5 2.0 convert_reduce_fusion.3
  223.5 58.2 %collective-permute-done.24 = f32[3072]{0:T(1024)S(1)} collective-permute-done((f32[3072]{0:T(1024)S(1)}, f32[3072]{0:T(1024)S(1)}, u32[]{:S(2)}, u32[]{:S(2)}) %collective-permute-start.24) | collective-permute-done | bytes 12320 | tf_op jit(solution)/shard_map/ppermute | solution.py:334
  281.7 1.7 collective-permute-start.25
  283.9 1.7 collective-permute-start.29
  285.7 2.9 convert_add_fusion.1
  289.4 16.6 %collective-permute-done.29 = f32[6144]{0:T(1024)S(1)} collective-permute-done((f32[6144]{0:T(1024)S(1)}, f32[6144]{0:T(1024)S(1)}, u32[]{:S(2)}, u32[]{:S(2)}) %collective-permute-start.29) | collective-permute-done | bytes 24608 | tf_op jit(solution)/shard_map/ppermute | solution.py:334
  307.5 2.3 collective-permute-done.30
  310.4 4.2 %collective-permute-done.31 = f32[6144]{0:T(1024)S(1)} collective-permute-done((f32[6144]{0:T(1024)S(1)}, f32[6144]{0:T(1024)S(1)}, u32[]{:S(2)}, u32[]{:S(2)}) %collective-permute-start.31) | collective-permute-done | bytes 24608 | tf_op jit(solution)/shard_map/ppermute | solution.py:334
  317.1 2.3 bitcast_add_fusion.1
  319.7 7.6 %collective-permute-done.41 = bf16[4,1,64,2048]{3,2,0,1:T(8,128)(2,1)} collective-permute-done((bf16[4,1,64,2048]{3,2,0,1:T(8,128)(2,1)}, bf16[4,1,64,2048]{3,2,0,1:T(8,128)(2,1)}, u32[]{:S(2)}, u32[]{:S(2)}) %collective-permute-start.41) | collective-permute-done | bytes 1048608 | tf_op jit(solution)/shard_map/ppermute | solution.py:328
  327.4 1.6 bitcast_add_fusion.2
  329.6 2.5 convert_add_fusion.2
  334.8 11.3 %collective-permute-done.42 = bf16[2,1,64,2048]{3,2,0,1:T(8,128)(2,1)S(1)} collective-permute-done((bf16[2,1,64,2048]{3,2,0,1:T(8,128)(2,1)S(1)}, bf16[2,1,64,2048]{3,2,0,1:T(8,128)(2,1)S(1)}, u32[]{:S(2)}, u32[]{:S(2)}) %collective-permute-start.42) | collective-permute-done | bytes 524320 | tf_op jit(solution)/shard_map/ppermute | solution.py:328
  350.2 10.5 %collective-permute-done.34 = bf16[2,1,64,1536]{3,2,0,1:T(8,128)(2,1)S(1)} collective-permute-done((bf16[2,1,64,1536]{3,2,0,1:T(8,128)(2,1)S(1)}, bf16[2,1,64,1536]{3,2,0,1:T(8,128)(2,1)S(1)}, u32[]{:S(2)}, u32[]{:S(2)}) %collective-permute-start.34) | collective-permute-done | bytes 393248 | tf_op jit(solution)/shard_map/ppermute | solution.py:328
  361.8 7.8 %collective-permute-done.35 = bf16[1,1,64,1536]{3,2,0,1:T(8,128)(2,1)S(1)} collective-permute-done((bf16[1,1,64,1536]{3,2,0,1:T(8,128)(2,1)S(1)}, bf16[1,1,64,1536]{3,2,0,1:T(8,128)(2,1)S(1)}, u32[]{:S(2)}, u32[]{:S(2)}) %collective-permute-start.35) | collective-permute-done | bytes 196640 | tf_op jit(solution)/shard_map/ppermute | solution.py:328
  (252 shorter events, 55.4 us)
Async XLA Ops:
  0.6 73.4 %copy-start = (bf16[512,1024]{1,0:T(8,128)(2,1)S(1)}, bf16[512,1024]{1,0:T(8,128)(2,1)}, u32[]{:S(2)}) copy-start(bf16[512,1024]{1,0:T(8,128)(2,1)} %param.23) | copy-start | bytes 3145732
  7.8 9.5 %copy-start.44 = (f32[4]{0:T(128)S(1)}, f32[4]{0:T(128)}, u32[]{:S(2)}) copy-start(f32[4]{0:T(128)} %param.18) | copy-start | bytes 52
  8.7 13.3 %collective-permute-start = (bf16[3,384,128]{2,1,0:T(8,128)(2,1)}, bf16[3,384,128]{2,1,0:T(8,128)(2,1)}, u32[]{:S(2)}, u32[]{:S(2)}) collective-permute-start(bf16[3,384,128]{2,1,0:T(8,128)(2,1)} %get-tuple-element.75), channel_id=1, source_target_pairs={{0,4},{4,8},{8,12},{12,0},{1,5},{5,9},{9,13},{13,1},{2,6},{6,10},{... | collective-permute-start | bytes 884744 | tf_op jit(solution)/shard_map/ppermute | solution.py:285
  11.8 22.1 %collective-permute-start.1 = (bf16[3,384,128]{2,1,0:T(8,128)(2,1)}, bf16[3,384,128]{2,1,0:T(8,128)(2,1)}, u32[]{:S(2)}, u32[]{:S(2)}) collective-permute-start(bf16[3,384,128]{2,1,0:T(8,128)(2,1)} %get-tuple-element.74), channel_id=1, source_target_pairs={{0,8},{4,12},{8,0},{12,4},{1,9},{5,13},{9,1},{13,5},{2,10},{6,14},... | collective-permute-start | bytes 884744 | tf_op jit(solution)/shard_map/ppermute | solution.py:285
  14.4 22.1 %collective-permute-start.2 = (bf16[3,384,128]{2,1,0:T(8,128)(2,1)S(1)}, bf16[3,384,128]{2,1,0:T(8,128)(2,1)}, u32[]{:S(2)}, u32[]{:S(2)}) collective-permute-start(bf16[3,384,128]{2,1,0:T(8,128)(2,1)S(1)} %get-tuple-element.73), channel_id=1, source_target_pairs={{0,12},{4,0},{8,4},{12,8},{1,13},{5,1},{9,5},{13,9},{2,14},{6,2},{... | collective-permute-start | bytes 884744 | tf_op jit(solution)/shard_map/ppermute | solution.py:285
  15.7 22.8 %collective-permute-start.3 = (bf16[2,384,128]{2,1,0:T(8,128)(2,1)S(1)}, bf16[2,384,128]{2,1,0:T(8,128)(2,1)S(1)}, u32[]{:S(2)}, u32[]{:S(2)}) collective-permute-start(bf16[2,384,128]{2,1,0:T(8,128)(2,1)S(1)} %dynamic-slice_bitcast_fusion.4), channel_id=1, source_target_pairs={{0,2},{2,0},{1,3},{3,1},{4,6},{6,4},{5,7},{7,5},{8,10},{10,8},{9,1... | collective-permute-start | bytes 589832 | tf_op jit(solution)/shard_map/ppermute | solution.py:285
  23.0 15.5 %collective-permute-start.4 = (bf16[2,384,128]{2,1,0:T(8,128)(2,1)S(1)}, bf16[2,384,128]{2,1,0:T(8,128)(2,1)S(1)}, u32[]{:S(2)}, u32[]{:S(2)}) collective-permute-start(bf16[2,384,128]{2,1,0:T(8,128)(2,1)S(1)} %slice.170), channel_id=1, source_target_pairs={{0,2},{2,0},{1,3},{3,1},{4,6},{6,4},{5,7},{7,5},{8,10},{10,8},{9,1... | collective-permute-start | bytes 589832 | tf_op jit(solution)/shard_map/ppermute | solution.py:285
  34.8 7.8 %collective-permute-start.5 = (bf16[2,384,128]{2,1,0:T(8,128)(2,1)S(1)}, bf16[2,384,128]{2,1,0:T(8,128)(2,1)S(1)}, u32[]{:S(2)}, u32[]{:S(2)}) collective-permute-start(bf16[2,384,128]{2,1,0:T(8,128)(2,1)S(1)} %slice.171), channel_id=1, source_target_pairs={{0,2},{2,0},{1,3},{3,1},{4,6},{6,4},{5,7},{7,5},{8,10},{10,8},{9,1... | collective-permute-start | bytes 589832 | tf_op jit(solution)/shard_map/ppermute | solution.py:285
  37.4 8.5 %collective-permute-start.6 = (bf16[2,384,128]{2,1,0:T(8,128)(2,1)S(1)}, bf16[2,384,128]{2,1,0:T(8,128)(2,1)S(1)}, u32[]{:S(2)}, u32[]{:S(2)}) collective-permute-start(bf16[2,384,128]{2,1,0:T(8,128)(2,1)S(1)} %slice.172), channel_id=1, source_target_pairs={{0,2},{2,0},{1,3},{3,1},{4,6},{6,4},{5,7},{7,5},{8,10},{10,8},{9,1... | collective-permute-start | bytes 589832 | tf_op jit(solution)/shard_map/ppermute | solution.py:285
  58.7 10.4 %collective-permute-start.7 = (bf16[384,128]{1,0:T(8,128)(2,1)}, bf16[384,128]{1,0:T(8,128)(2,1)S(1)}, u32[]{:S(2)}, u32[]{:S(2)}) collective-permute-start(bf16[384,128]{1,0:T(8,128)(2,1)} %get-tuple-element.25), channel_id=1, source_target_pairs={{0,4},{4,8},{8,12},{12,0},{1,5},{5,9},{9,13},{13,1},{2,6},{6,10},{... | collective-permute-start | bytes 294920 | tf_op jit(solution)/shard_map/ppermute | solution.py:285
  62.8 9.2 %collective-permute-start.8 = (bf16[384,128]{1,0:T(8,128)(2,1)}, bf16[384,128]{1,0:T(8,128)(2,1)S(1)}, u32[]{:S(2)}, u32[]{:S(2)}) collective-permute-start(bf16[384,128]{1,0:T(8,128)(2,1)} %get-tuple-element.26), channel_id=1, source_target_pairs={{0,8},{4,12},{8,0},{12,4},{1,9},{5,13},{9,1},{13,5},{2,10},{6,14},... | collective-permute-start | bytes 294920 | tf_op jit(solution)/shard_map/ppermute | solution.py:285
  66.1 6.0 %collective-permute-start.9 = (bf16[384,128]{1,0:T(8,128)(2,1)}, bf16[384,128]{1,0:T(8,128)(2,1)S(1)}, u32[]{:S(2)}, u32[]{:S(2)}) collective-permute-start(bf16[384,128]{1,0:T(8,128)(2,1)} %get-tuple-element.27), channel_id=1, source_target_pairs={{0,12},{4,0},{8,4},{12,8},{1,13},{5,1},{9,5},{13,9},{2,14},{6,2},{... | collective-permute-start | bytes 294920 | tf_op jit(solution)/shard_map/ppermute | solution.py:285
  75.6 8.8 %collective-permute-start.10 = (bf16[384,1024]{1,0:T(8,128)(2,1)}, bf16[384,1024]{1,0:T(8,128)(2,1)}, u32[]{:S(2)}, u32[]{:S(2)}) collective-permute-start(bf16[384,1024]{1,0:T(8,128)(2,1)} %convolution_convert_fusion.6), channel_id=1, source_target_pairs={{0,1},{1,0},{2,3},{3,2},{4,5},{5,4},{6,7},{7,6},{8,9},{9,8},{10,11... | collective-permute-start | bytes 2359304 | tf_op jit(solution)/shard_map/ppermute | solution.py:285
  87.4 14.0 %copy-start.14 = (bf16[384,1024]{1,0:T(8,128)(2,1)}, bf16[384,1024]{1,0:T(8,128)(2,1)S(1)}, u32[]{:S(2)}) copy-start(bf16[384,1024]{1,0:T(8,128)(2,1)S(1)} %add_convert_fusion.2) | copy-start | bytes 2359300
  91.9 9.5 %copy-start.21 = (bf16[384,2048]{1,0:T(8,128)(2,1)}, bf16[384,2048]{1,0:T(8,128)(2,1)S(1)}, u32[]{:S(2)}) copy-start(bf16[384,2048]{1,0:T(8,128)(2,1)S(1)} %get-tuple-element.65) | copy-start | bytes 4718596
  93.8 10.3 %collective-permute-start.12 = (bf16[384,1024]{1,0:T(8,128)(2,1)S(1)}, bf16[384,1024]{1,0:T(8,128)(2,1)S(1)}, u32[]{:S(2)}, u32[]{:S(2)}) collective-permute-start(bf16[384,1024]{1,0:T(8,128)(2,1)S(1)} %convolution_convert_fusion.4), channel_id=1, source_target_pairs={{0,1},{1,0},{2,3},{3,2},{4,5},{5,4},{6,7},{7,6},{8,9},{9,8},{10,11... | collective-permute-start | bytes 2359304 | tf_op jit(solution)/shard_map/ppermute | solution.py:285
  97.9 6.9 %collective-permute-start.11 = (bf16[384,1024]{1,0:T(8,128)(2,1)S(1)}, bf16[384,1024]{1,0:T(8,128)(2,1)S(1)}, u32[]{:S(2)}, u32[]{:S(2)}) collective-permute-start(bf16[384,1024]{1,0:T(8,128)(2,1)S(1)} %convolution_convert_fusion.5), channel_id=1, source_target_pairs={{0,1},{1,0},{2,3},{3,2},{4,5},{5,4},{6,7},{7,6},{8,9},{9,8},{10,11... | collective-permute-start | bytes 2359304 | tf_op jit(solution)/shard_map/ppermute | solution.py:285
  108.9 38.7 %collective-permute-start.36 = (bf16[512,512]{1,0:T(8,128)(2,1)}, bf16[512,512]{1,0:T(8,128)(2,1)}, u32[]{:S(2)}, u32[]{:S(2)}) collective-permute-start(bf16[512,512]{1,0:T(8,128)(2,1)} %convolution_convert_fusion.7), channel_id=1, source_target_pairs={{0,16},{16,0},{1,17},{17,1},{2,18},{18,2},{3,19},{19,3},{4,20},{20... | collective-permute-start | bytes 1572872 | tf_op jit(solution)/shard_map/ppermute | solution.py:285
  111.7 5.7 %collective-permute-start.13 = (bf16[384,128]{1,0:T(8,128)(2,1)S(1)}, bf16[384,128]{1,0:T(8,128)(2,1)S(1)}, u32[]{:S(2)}, u32[]{:S(2)}) collective-permute-start(bf16[384,128]{1,0:T(8,128)(2,1)S(1)} %get-tuple-element.86), channel_id=1, source_target_pairs={{0,12},{4,0},{8,4},{12,8},{1,13},{5,1},{9,5},{13,9},{2,14},{6,2},{... | collective-permute-start | bytes 294920 | tf_op jit(solution)/shard_map/ppermute | solution.py:285
  114.2 9.4 %collective-permute-start.14 = (bf16[384,128]{1,0:T(8,128)(2,1)S(1)}, bf16[384,128]{1,0:T(8,128)(2,1)S(1)}, u32[]{:S(2)}, u32[]{:S(2)}) collective-permute-start(bf16[384,128]{1,0:T(8,128)(2,1)S(1)} %get-tuple-element.85), channel_id=1, source_target_pairs={{0,8},{4,12},{8,0},{12,4},{1,9},{5,13},{9,1},{13,5},{2,10},{6,14},... | collective-permute-start | bytes 294920 | tf_op jit(solution)/shard_map/ppermute | solution.py:285
  114.8 8.8 %collective-permute-start.15 = (bf16[384,128]{1,0:T(8,128)(2,1)S(1)}, bf16[384,128]{1,0:T(8,128)(2,1)S(1)}, u32[]{:S(2)}, u32[]{:S(2)}) collective-permute-start(bf16[384,128]{1,0:T(8,128)(2,1)S(1)} %get-tuple-element.84), channel_id=1, source_target_pairs={{0,4},{4,8},{8,12},{12,0},{1,5},{5,9},{9,13},{13,1},{2,6},{6,10},{... | collective-permute-start | bytes 294920 | tf_op jit(solution)/shard_map/ppermute | solution.py:285
  140.7 9.4 %copy-start.39 = (bf16[384,128]{1,0:T(8,128)(2,1)S(1)}, bf16[384,128]{1,0:T(8,128)(2,1)}, u32[]{:S(2)}) copy-start(bf16[384,128]{1,0:T(8,128)(2,1)} %get-tuple-element.31) | copy-start | bytes 294916
  140.7 9.4 %copy-start.38 = (bf16[384,128]{1,0:T(8,128)(2,1)S(1)}, bf16[384,128]{1,0:T(8,128)(2,1)}, u32[]{:S(2)}) copy-start(bf16[384,128]{1,0:T(8,128)(2,1)} %get-tuple-element.32) | copy-start | bytes 294916
  140.7 11.2 %copy-start.37 = (bf16[384,128]{1,0:T(8,128)(2,1)S(1)}, bf16[384,128]{1,0:T(8,128)(2,1)}, u32[]{:S(2)}) copy-start(bf16[384,128]{1,0:T(8,128)(2,1)} %get-tuple-element.33) | copy-start | bytes 294916
  140.7 20.0 %copy-start.23 = (bf16[384,128]{1,0:T(8,128)(2,1)S(1)}, bf16[384,128]{1,0:T(8,128)(2,1)}, u32[]{:S(2)}) copy-start(bf16[384,128]{1,0:T(8,128)(2,1)} %get-tuple-element.30) | copy-start | bytes 294916
  140.8 31.1 %collective-permute-start.19 = (bf16[4,2,384,128]{3,2,1,0:T(8,128)(2,1)}, bf16[4,2,384,128]{3,2,1,0:T(8,128)(2,1)}, u32[]{:S(2)}, u32[]{:S(2)}) collective-permute-start(bf16[4,2,384,128]{3,2,1,0:T(8,128)(2,1)} %bitcast.226), channel_id=1, source_target_pairs={{0,2},{2,0},{1,3},{3,1},{4,6},{6,4},{5,7},{7,5},{8,10},{10,8},{9,1... | collective-permute-start | bytes 2359304 | tf_op jit(solution)/shard_map/ppermute | solution.py:285
  150.0 20.7 %collective-permute-start.37 = (bf16[4,1,64,512]{3,2,0,1:T(8,128)(2,1)}, bf16[4,1,64,512]{3,2,0,1:T(8,128)(2,1)}, u32[]{:S(2)}, u32[]{:S(2)}) collective-permute-start(bf16[4,1,64,512]{3,2,0,1:T(8,128)(2,1)} %fusion.56), channel_id=1, source_target_pairs={{0,2},{2,0},{1,3},{3,1},{4,6},{6,4},{5,7},{7,5},{8,10},{10,8},{9,1... | collective-permute-start | bytes 786440 | tf_op jit(solution)/shard_map/ppermute | solution.py:328
  150.1 7.5 %collective-permute-start.16 = (bf16[384,128]{1,0:T(8,128)(2,1)S(1)}, bf16[384,128]{1,0:T(8,128)(2,1)S(1)}, u32[]{:S(2)}, u32[]{:S(2)}) collective-permute-start(bf16[384,128]{1,0:T(8,128)(2,1)S(1)} %copy-done.39), channel_id=1, source_target_pairs={{0,4},{4,8},{8,12},{12,0},{1,5},{5,9},{9,13},{13,1},{2,6},{6,10},{... | collective-permute-start | bytes 294920 | tf_op jit(solution)/shard_map/ppermute | solution.py:285
  150.1 10.1 %collective-permute-start.17 = (bf16[384,128]{1,0:T(8,128)(2,1)S(1)}, bf16[384,128]{1,0:T(8,128)(2,1)S(1)}, u32[]{:S(2)}, u32[]{:S(2)}) collective-permute-start(bf16[384,128]{1,0:T(8,128)(2,1)S(1)} %copy-done.38), channel_id=1, source_target_pairs={{0,8},{4,12},{8,0},{12,4},{1,9},{5,13},{9,1},{13,5},{2,10},{6,14},... | collective-permute-start | bytes 294920 | tf_op jit(solution)/shard_map/ppermute | solution.py:285
  151.9 8.8 %collective-permute-start.18 = (bf16[384,128]{1,0:T(8,128)(2,1)S(1)}, bf16[384,128]{1,0:T(8,128)(2,1)S(1)}, u32[]{:S(2)}, u32[]{:S(2)}) collective-permute-start(bf16[384,128]{1,0:T(8,128)(2,1)S(1)} %copy-done.37), channel_id=1, source_target_pairs={{0,12},{4,0},{8,4},{12,8},{1,13},{5,1},{9,5},{13,9},{2,14},{6,2},{... | collective-permute-start | bytes 294920 | tf_op jit(solution)/shard_map/ppermute | solution.py:285
  157.6 56.8 %collective-permute-start.44 = (bf16[512,2048]{1,0:T(8,128)(2,1)}, bf16[512,2048]{1,0:T(8,128)(2,1)}, u32[]{:S(2)}, u32[]{:S(2)}) collective-permute-start(bf16[512,2048]{1,0:T(8,128)(2,1)} %convolution_convert_fusion), channel_id=1, source_target_pairs={{0,16},{16,0},{1,17},{17,1},{2,18},{18,2},{3,19},{19,3},{4,20},{20... | collective-permute-start | bytes 6291464 | tf_op jit(solution)/shard_map/ppermute | solution.py:285
  160.2 125.5 %collective-permute-start.40 = (bf16[512,2048]{1,0:T(8,128)(2,1)}, bf16[512,2048]{1,0:T(8,128)(2,1)}, u32[]{:S(2)}, u32[]{:S(2)}) collective-permute-start(bf16[512,2048]{1,0:T(8,128)(2,1)} %convolution_convert_fusion.1), channel_id=1, source_target_pairs={{0,16},{16,0},{1,17},{17,1},{2,18},{18,2},{3,19},{19,3},{4,20},{20... | collective-permute-start | bytes 6291464 | tf_op jit(solution)/shard_map/ppermute | solution.py:285
  171.8 5.0 %collective-permute-start.38 = (bf16[2,1,64,512]{3,2,0,1:T(8,128)(2,1)S(1)}, bf16[2,1,64,512]{3,2,0,1:T(8,128)(2,1)S(1)}, u32[]{:S(2)}, u32[]{:S(2)}) collective-permute-start(bf16[2,1,64,512]{3,2,0,1:T(8,128)(2,1)S(1)} %fusion.57), channel_id=1, source_target_pairs={{0,4},{4,0},{8,12},{12,8},{1,5},{5,1},{9,13},{13,9},{2,6},{6,2},{1... | collective-permute-start | bytes 393224 | tf_op jit(solution)/shard_map/ppermute | solution.py:328
  176.9 12.3 %collective-permute-start.39 = (bf16[1,1,64,512]{3,2,0,1:T(8,128)(2,1)S(1)}, bf16[1,1,64,512]{3,2,0,1:T(8,128)(2,1)S(1)}, u32[]{:S(2)}, u32[]{:S(2)}) collective-permute-start(bf16[1,1,64,512]{3,2,0,1:T(8,128)(2,1)S(1)} %dynamic-slice_convert_fusion.7), channel_id=1, source_target_pairs={{0,8},{4,12},{8,0},{12,4},{1,9},{5,13},{9,1},{13,5},{2,10},{6,14},... | collective-permute-start | bytes 196616 | tf_op jit(solution)/shard_map/ppermute | solution.py:328
  178.0 12.2 %collective-permute-start.20 = (bf16[2,384,128]{2,1,0:T(8,128)(2,1)S(1)}, bf16[2,384,128]{2,1,0:T(8,128)(2,1)S(1)}, u32[]{:S(2)}, u32[]{:S(2)}) collective-permute-start(bf16[2,384,128]{2,1,0:T(8,128)(2,1)S(1)} %get-tuple-element.81), channel_id=1, source_target_pairs={{0,4},{4,8},{8,12},{12,0},{1,5},{5,9},{9,13},{13,1},{2,6},{6,10},{... | collective-permute-start | bytes 589832 | tf_op jit(solution)/shard_map/ppermute | solution.py:285
  178.0 16.7 %collective-permute-start.21 = (bf16[2,384,128]{2,1,0:T(8,128)(2,1)S(1)}, bf16[2,384,128]{2,1,0:T(8,128)(2,1)S(1)}, u32[]{:S(2)}, u32[]{:S(2)}) collective-permute-start(bf16[2,384,128]{2,1,0:T(8,128)(2,1)S(1)} %get-tuple-element.83), channel_id=1, source_target_pairs={{0,8},{4,12},{8,0},{12,4},{1,9},{5,13},{9,1},{13,5},{2,10},{6,14},... | collective-permute-start | bytes 589832 | tf_op jit(solution)/shard_map/ppermute | solution.py:285
  189.2 6.8 %collective-permute-start.22 = (bf16[2,384,128]{2,1,0:T(8,128)(2,1)S(1)}, bf16[2,384,128]{2,1,0:T(8,128)(2,1)S(1)}, u32[]{:S(2)}, u32[]{:S(2)}) collective-permute-start(bf16[2,384,128]{2,1,0:T(8,128)(2,1)S(1)} %get-tuple-element.82), channel_id=1, source_target_pairs={{0,12},{4,0},{8,4},{12,8},{1,13},{5,1},{9,5},{13,9},{2,14},{6,2},{... | collective-permute-start | bytes 589832 | tf_op jit(solution)/shard_map/ppermute | solution.py:285
  210.9 6.8 %collective-permute-start.23 = (bf16[384,1024]{1,0:T(8,128)(2,1)S(1)}, bf16[384,1024]{1,0:T(8,128)(2,1)S(1)}, u32[]{:S(2)}, u32[]{:S(2)}) collective-permute-start(bf16[384,1024]{1,0:T(8,128)(2,1)S(1)} %convolution_convert_fusion.3), channel_id=1, source_target_pairs={{0,1},{1,0},{2,3},{3,2},{4,5},{5,4},{6,7},{7,6},{8,9},{9,8},{10,11... | collective-permute-start | bytes 2359304 | tf_op jit(solution)/shard_map/ppermute | solution.py:285
  213.5 116.0 %collective-permute-start.32 = (bf16[512,1536]{1,0:T(8,128)(2,1)}, bf16[512,1536]{1,0:T(8,128)(2,1)}, u32[]{:S(2)}, u32[]{:S(2)}) collective-permute-start(bf16[512,1536]{1,0:T(8,128)(2,1)} %convolution_convert_fusion.2), channel_id=1, source_target_pairs={{0,16},{16,0},{1,17},{17,1},{2,18},{18,2},{3,19},{19,3},{4,20},{20... | collective-permute-start | bytes 4718600 | tf_op jit(solution)/shard_map/ppermute | solution.py:285
  217.7 65.7 %copy-start.13 = (f32[512,2048]{1,0:T(8,128)}, f32[512,2048]{1,0:T(8,128)S(1)}, u32[]{:S(2)}) copy-start(f32[512,2048]{1,0:T(8,128)S(1)} %convert_add_fusion) | copy-start | bytes 12582916
  219.2 62.4 %collective-permute-start.24 = (f32[3072]{0:T(1024)S(1)}, f32[3072]{0:T(1024)S(1)}, u32[]{:S(2)}, u32[]{:S(2)}) collective-permute-start(f32[3072]{0:T(1024)S(1)} %pad_maximum_fusion.5), channel_id=1, source_target_pairs={{0,16},{16,0},{1,17},{17,1},{2,18},{18,2},{3,19},{19,3},{4,20},{20... | collective-permute-start | bytes 36872 | tf_op jit(solution)/shard_map/ppermute | solution.py:334
  220.5 65.2 %copy-start.22 = (bf16[384,2048]{1,0:T(8,128)(2,1)S(1)}, bf16[384,2048]{1,0:T(8,128)(2,1)}, u32[]{:S(2)}) copy-start(bf16[384,2048]{1,0:T(8,128)(2,1)} %copy-done.21) | copy-start | bytes 4718596
  222.6 63.1 %copy-start.15 = (bf16[384,1024]{1,0:T(8,128)(2,1)S(1)}, bf16[384,1024]{1,0:T(8,128)(2,1)}, u32[]{:S(2)}) copy-start(bf16[384,1024]{1,0:T(8,128)(2,1)} %copy-done.14) | copy-start | bytes 2359300
  222.6 61.3 %collective-permute-start.28 = (f32[6144]{0:T(1024)S(1)}, f32[6144]{0:T(1024)S(1)}, u32[]{:S(2)}, u32[]{:S(2)}) collective-permute-start(f32[6144]{0:T(1024)S(1)} %constant_dynamic-update-slice_fusion), channel_id=1, source_target_pairs={{0,16},{16,0},{1,17},{17,1},{2,18},{18,2},{3,19},{19,3},{4,20},{20... | collective-permute-start | bytes 73736 | tf_op jit(solution)/shard_map/ppermute | solution.py:334
  281.7 4.0 %collective-permute-start.25 = (f32[3072]{0:T(1024)S(1)}, f32[3072]{0:T(1024)S(1)}, u32[]{:S(2)}, u32[]{:S(2)}) collective-permute-start(f32[3072]{0:T(1024)S(1)} %fusion.69), channel_id=1, source_target_pairs={{0,2},{2,0},{1,3},{3,1},{4,6},{6,4},{5,7},{7,5},{8,10},{10,8},{9,1... | collective-permute-start | bytes 36872 | tf_op jit(solution)/shard_map/ppermute | solution.py:334
  283.5 33.6 %collective-permute-start.45 = (bf16[4,1,64,2048]{3,2,0,1:T(8,128)(2,1)S(1)}, bf16[4,1,64,2048]{3,2,0,1:T(8,128)(2,1)}, u32[]{:S(2)}, u32[]{:S(2)}) collective-permute-start(bf16[4,1,64,2048]{3,2,0,1:T(8,128)(2,1)S(1)} %fusion.29), channel_id=1, source_target_pairs={{0,2},{2,0},{1,3},{3,1},{4,6},{6,4},{5,7},{7,5},{8,10},{10,8},{9,1... | collective-permute-start | bytes 3145736 | tf_op jit(solution)/shard_map/ppermute | solution.py:328
  283.9 22.0 %collective-permute-start.29 = (f32[6144]{0:T(1024)S(1)}, f32[6144]{0:T(1024)S(1)}, u32[]{:S(2)}, u32[]{:S(2)}) collective-permute-start(f32[6144]{0:T(1024)S(1)} %add.375), channel_id=1, source_target_pairs={{0,2},{2,0},{1,3},{3,1},{4,6},{6,4},{5,7},{7,5},{8,10},{10,8},{9,1... | collective-permute-start | bytes 73736 | tf_op jit(solution)/shard_map/ppermute | solution.py:334
  285.7 3.7 collective-permute-start.26
  288.6 17.3 %copy-start.3 = (f32[512,2048]{1,0:T(8,128)}, f32[512,2048]{1,0:T(8,128)S(1)}, u32[]{:S(2)}) copy-start(f32[512,2048]{1,0:T(8,128)S(1)} %convert_add_fusion.1) | copy-start | bytes 12582916
  289.4 18.1 %collective-permute-start.27 = (f32[3072]{0:T(1024)S(1)}, f32[3072]{0:T(1024)S(1)}, u32[]{:S(2)}, u32[]{:S(2)}) collective-permute-start(f32[3072]{0:T(1024)S(1)} %add.373), channel_id=1, source_target_pairs={{0,8},{4,12},{8,0},{12,4},{1,9},{5,13},{9,1},{13,5},{2,10},{6,14},... | collective-permute-start | bytes 36872 | tf_op jit(solution)/shard_map/ppermute | solution.py:334
  306.0 3.8 %collective-permute-start.30 = (f32[6144]{0:T(1024)S(1)}, f32[6144]{0:T(1024)S(1)}, u32[]{:S(2)}, u32[]{:S(2)}) collective-permute-start(f32[6144]{0:T(1024)S(1)} %add.376), channel_id=1, source_target_pairs={{0,4},{4,0},{8,12},{12,8},{1,5},{5,1},{9,13},{13,9},{2,6},{6,2},{1... | collective-permute-start | bytes 73736 | tf_op jit(solution)/shard_map/ppermute | solution.py:334
  307.1 20.2 %collective-permute-start.41 = (bf16[4,1,64,2048]{3,2,0,1:T(8,128)(2,1)}, bf16[4,1,64,2048]{3,2,0,1:T(8,128)(2,1)}, u32[]{:S(2)}, u32[]{:S(2)}) collective-permute-start(bf16[4,1,64,2048]{3,2,0,1:T(8,128)(2,1)} %fusion.28), channel_id=1, source_target_pairs={{0,2},{2,0},{1,3},{3,1},{4,6},{6,4},{5,7},{7,5},{8,10},{10,8},{9,1... | collective-permute-start | bytes 3145736 | tf_op jit(solution)/shard_map/ppermute | solution.py:328
  309.8 4.8 %collective-permute-start.31 = (f32[6144]{0:T(1024)S(1)}, f32[6144]{0:T(1024)S(1)}, u32[]{:S(2)}, u32[]{:S(2)}) collective-permute-start(f32[6144]{0:T(1024)S(1)} %add.377), channel_id=1, source_target_pairs={{0,8},{4,12},{8,0},{12,4},{1,9},{5,13},{9,1},{13,5},{2,10},{6,14},... | collective-permute-start | bytes 73736 | tf_op jit(solution)/shard_map/ppermute | solution.py:334
  317.1 10.3 %copy-start.4 = (f32[512,2048]{1,0:T(8,128)S(1)}, f32[512,2048]{1,0:T(8,128)}, u32[]{:S(2)}) copy-start(f32[512,2048]{1,0:T(8,128)} %copy-done.3) | copy-start | bytes 12582916
  319.5 10.1 %copy-start.8 = (bf16[384,4,128]{0,2,1:T(8,128)(2,1)S(1)}, bf16[384,4,128]{0,2,1:T(8,128)(2,1)}, u32[]{:S(2)}) copy-start(bf16[384,4,128]{0,2,1:T(8,128)(2,1)} %copy.45) | copy-start | bytes 1179652
  319.5 10.1 %copy-start.18 = (bf16[384,1024]{1,0:T(8,128)(2,1)S(1)}, bf16[384,1024]{1,0:T(8,128)(2,1)}, u32[]{:S(2)}) copy-start(bf16[384,1024]{1,0:T(8,128)(2,1)} %copy-done.16) | copy-start | bytes 2359300
  319.5 15.1 %collective-permute-start.46 = (bf16[2,1,64,2048]{3,2,0,1:T(8,128)(2,1)S(1)}, bf16[2,1,64,2048]{3,2,0,1:T(8,128)(2,1)S(1)}, u32[]{:S(2)}, u32[]{:S(2)}) collective-permute-start(bf16[2,1,64,2048]{3,2,0,1:T(8,128)(2,1)S(1)} %fusion.34), channel_id=1, source_target_pairs={{0,4},{4,0},{8,12},{12,8},{1,5},{5,1},{9,13},{13,9},{2,6},{6,2},{1... | collective-permute-start | bytes 1572872 | tf_op jit(solution)/shard_map/ppermute | solution.py:328
  329.0 17.2 %collective-permute-start.42 = (bf16[2,1,64,2048]{3,2,0,1:T(8,128)(2,1)S(1)}, bf16[2,1,64,2048]{3,2,0,1:T(8,128)(2,1)S(1)}, u32[]{:S(2)}, u32[]{:S(2)}) collective-permute-start(bf16[2,1,64,2048]{3,2,0,1:T(8,128)(2,1)S(1)} %fusion.33), channel_id=1, source_target_pairs={{0,4},{4,0},{8,12},{12,8},{1,5},{5,1},{9,13},{13,9},{2,6},{6,2},{1... | collective-permute-start | bytes 1572872 | tf_op jit(solution)/shard_map/ppermute | solution.py:328
  332.1 14.3 %collective-permute-start.33 = (bf16[4,1,64,1536]{3,2,0,1:T(8,128)(2,1)S(1)}, bf16[4,1,64,1536]{3,2,0,1:T(8,128)(2,1)S(1)}, u32[]{:S(2)}, u32[]{:S(2)}) collective-permute-start(bf16[4,1,64,1536]{3,2,0,1:T(8,128)(2,1)S(1)} %fusion.31), channel_id=1, source_target_pairs={{0,2},{2,0},{1,3},{3,1},{4,6},{6,4},{5,7},{7,5},{8,10},{10,8},{9,1... | collective-permute-start | bytes 2359304 | tf_op jit(solution)/shard_map/ppermute | solution.py:328
  334.8 14.6 %collective-permute-start.47 = (bf16[1,1,64,2048]{3,2,0,1:T(8,128)(2,1)S(1)}, bf16[1,1,64,2048]{3,2,0,1:T(8,128)(2,1)S(1)}, u32[]{:S(2)}, u32[]{:S(2)}) collective-permute-start(bf16[1,1,64,2048]{3,2,0,1:T(8,128)(2,1)S(1)} %dynamic-slice_convert_fusion.3), channel_id=1, source_target_pairs={{0,8},{4,12},{8,0},{12,4},{1,9},{5,13},{9,1},{13,5},{2,10},{6,14},... | collective-permute-start | bytes 786440 | tf_op jit(solution)/shard_map/ppermute | solution.py:328
  346.4 14.6 %collective-permute-start.43 = (bf16[1,1,64,2048]{3,2,0,1:T(8,128)(2,1)S(1)}, bf16[1,1,64,2048]{3,2,0,1:T(8,128)(2,1)S(1)}, u32[]{:S(2)}, u32[]{:S(2)}) collective-permute-start(bf16[1,1,64,2048]{3,2,0,1:T(8,128)(2,1)S(1)} %dynamic-slice_convert_fusion.4), channel_id=1, source_target_pairs={{0,8},{4,12},{8,0},{12,4},{1,9},{5,13},{9,1},{13,5},{2,10},{6,14},... | collective-permute-start | bytes 786440 | tf_op jit(solution)/shard_map/ppermute | solution.py:328
  346.7 14.0 %collective-permute-start.34 = (bf16[2,1,64,1536]{3,2,0,1:T(8,128)(2,1)S(1)}, bf16[2,1,64,1536]{3,2,0,1:T(8,128)(2,1)S(1)}, u32[]{:S(2)}, u32[]{:S(2)}) collective-permute-start(bf16[2,1,64,1536]{3,2,0,1:T(8,128)(2,1)S(1)} %fusion.35), channel_id=1, source_target_pairs={{0,4},{4,0},{8,12},{12,8},{1,5},{5,1},{9,13},{13,9},{2,6},{6,2},{1... | collective-permute-start | bytes 1179656 | tf_op jit(solution)/shard_map/ppermute | solution.py:328
  360.9 8.7 %collective-permute-start.35 = (bf16[1,1,64,1536]{3,2,0,1:T(8,128)(2,1)S(1)}, bf16[1,1,64,1536]{3,2,0,1:T(8,128)(2,1)S(1)}, u32[]{:S(2)}, u32[]{:S(2)}) collective-permute-start(bf16[1,1,64,1536]{3,2,0,1:T(8,128)(2,1)S(1)} %dynamic-slice_convert_fusion.5), channel_id=1, source_target_pairs={{0,8},{4,12},{8,0},{12,4},{1,9},{5,13},{9,1},{13,5},{2,10},{6,14},... | collective-permute-start | bytes 589832 | tf_op jit(solution)/shard_map/ppermute | solution.py:328
  361.0 9.9 %copy-start.1 = (bf16[512,1024]{1,0:T(8,128)(2,1)S(1)}, bf16[512,1024]{1,0:T(8,128)(2,1)}, u32[]{:S(2)}) copy-start(bf16[512,1024]{1,0:T(8,128)(2,1)} %param.23) | copy-start | bytes 3145732
  (32 other events, 123.9 us)
